TPU v7x, 32 devices: a whole 2x2x4 slice. The times are simulated.
32 devices in a mesh: groups: 2 (over y), replica: 4 (over z), tensor: 4 (over x, core).
Axes of the slice: x: 2, y: 2, z: 4, core: 2. Of those that a mesh axis runs over, the one named last changes fastest.
Arguments:
- queries: bfloat16 [512, 64, 128], P(('groups', 'replica'), 'tensor'), parts along dimension 0, may hold values from -256 to 256
- prefix_pool: bfloat16 [16, 64, 2, 8, 128], P(('groups', 'replica'), None, None, 'tensor'), parts along dimension 0, may hold values from -8 to 8
- page_table: int32 [12], P('groups'), parts along dimension 0, may hold values from 0 to 7, as said below
- suffix_kv: bfloat16 [512, 24, 2, 8, 128], P(('groups', 'replica'), None, None, 'tensor'), parts along dimension 0, may hold values from -9 to 9
- new_kv: bfloat16 [512, 2, 8, 128], P(('groups', 'replica'), None, 'tensor'), parts along dimension 0, may hold values from -10 to 10
- suffix_len: int32 [512], P(('groups', 'replica')), parts along dimension 0, may hold values from 0 to 24
- counts: int32 [8], P(('groups', 'replica')), parts along dimension 0, may hold values from 0 to 64, as said below
Outputs:
- attended: bfloat16 [512, 64, 128], P(('groups', 'replica'), 'tensor'), parts along dimension 0
There are 2 independent parts, one for each index of `groups`. A program takes and returns all parts, laid end to end along the dimension named above; each array names one. Nothing has to cross between parts.
Inputs may be any that keep to these rules, and one draw needn't show every extreme that they name: `page_table`: 6 distinct pool slots, among them slots 0 and 7. The counts of replicas 2i and 2i + 1 sum to 64.
All inputs are finite; a program needn't handle non-finite values.
Results may differ from a plain program's by a relative error of at most 0.013.
Values may be sent and summed in bfloat16 or wider, within the bound.
No kernel may reach another device: no remote copies, remote signals or barrier semaphores. Data moves between devices by JAX's collectives and lax.ppermute only.
A program may use at most 64 MiB of HBM per device.

v0:
```python
import functools
import math

import jax
import jax.numpy as jnp
from jax import lax
from jax.experimental import pallas as pl
from jax.experimental.pallas import tpu as pltpu
from jax.sharding import PartitionSpec as P

masked_score = -1e30
lanes = 128


def one_hot(shape, condition):
    row = lax.broadcasted_iota(jnp.int32, shape, 0)
    column = lax.broadcasted_iota(jnp.int32, shape, 1)
    return jnp.where(condition(row, column), 1.0, 0.0).astype(jnp.bfloat16)


def head_concat(grouped, heads, group):
    row = lax.broadcasted_iota(jnp.int32, grouped.shape, 0)
    head = lax.rem(row, heads * group) // group
    values = grouped.astype(jnp.float32)
    parts = [jnp.where(head == g, values, 0.0).astype(jnp.bfloat16) for g in range(heads)]
    return jnp.concatenate(parts, axis=1)


def head_select(wide, heads, group):
    width = wide.shape[1] // heads
    shape = (wide.shape[0], width)
    head = lax.rem(lax.broadcasted_iota(jnp.int32, shape, 0), heads * group) // group
    result = wide[:, :width]
    for g in range(1, heads):
        result = jnp.where(head == g, wide[:, g * width : (g + 1) * width], result)
    return result


def split_page(raw, order, heads):
    sorted_rows = jnp.dot(order, raw, preferred_element_type=jnp.float32).astype(jnp.bfloat16)
    tokens = raw.shape[0] // (2 * heads)
    kinds = [sorted_rows[i * tokens : (i + 1) * tokens] for i in range(2 * heads)]
    return jnp.concatenate(kinds[:heads], axis=1), jnp.concatenate(kinds[heads:], axis=1)


def page_order(page_rows, kinds):
    tokens = page_rows // kinds
    return one_hot(
        (page_rows, page_rows),
        lambda row, column: column == lax.rem(row, tokens) * kinds + row // tokens,
    )


def slot_bias(table_ref, slot):
    size = table_ref.shape[0]

    def look(index, found):
        return jnp.maximum(found, (table_ref[index] == slot).astype(jnp.int32))

    found = lax.fori_loop(0, size, look, jnp.int32(0), unroll=size <= 16)
    return jnp.where(found > 0, 0.0, masked_score)


def live_bias(table_ref, slots, page, rows):
    column = lax.broadcasted_iota(jnp.int32, (rows, len(slots) * page), 1)
    bias = jnp.zeros(column.shape, jnp.float32)
    for place, slot in enumerate(slots):
        bias = jnp.where(column // page == place, slot_bias(table_ref, slot), bias)
    return bias


def fill_tables(raws, order, keys_ref, values_ref, heads, page):
    place = 0
    page_rows = page * 2 * heads
    for raw_ref in raws:
        for at in range(0, raw_ref.shape[0], page_rows):
            keys, values = split_page(raw_ref[at : at + page_rows], order, heads)
            keys_ref[place : place + page] = keys
            values_ref[place : place + page] = values
            place += page


def contract_last(a, b):
    return lax.dot_general(a, b, (((1,), (1,)), ((), ())), preferred_element_type=jnp.float32)


def local_body(sizes, owners, *refs):
    heads, group, page, suffix, scale, batch, replicas, wave = sizes
    table_hbm, lens_hbm, q_hbm, own_hbm, suffix_hbm, new_hbm = refs[:6]
    acc_ref, max_ref, part_ref, wide_ref, bias_ref = refs[6:11]
    table_ref, lens_ref, q_ref, own_ref, suffix_ref, new_ref = refs[11:17]
    keys_ref, values_ref, sems = refs[17:]
    kinds = 2 * heads
    row_heads = heads * group
    cached = suffix * kinds
    fresh = batch * kinds
    width = cached + fresh
    batches = q_ref.shape[0] // (batch * row_heads)
    waves = batches // wave
    wave_rows = wave * batch * cached
    pairs = [
        (own_hbm, own_ref),
        (q_hbm, q_ref),
        (new_hbm, new_ref),
        (table_hbm, table_ref),
        (lens_hbm, lens_ref),
    ] + [
        (suffix_hbm.at[pl.ds(i * wave_rows, wave_rows)], suffix_ref.at[pl.ds(i * wave_rows, wave_rows)])
        for i in range(waves)
    ]
    copies = [
        pltpu.make_async_copy(source, target, sems.at[i])
        for i, (source, target) in enumerate(pairs)
    ]
    for copy in copies:
        copy.start()
    me = lax.axis_index("replica")
    slots = own_ref.shape[0] // (page * kinds)
    order = page_order(page * kinds, kinds)
    column = lax.broadcasted_iota(jnp.int32, (row_heads, width), 1)
    head = lax.broadcasted_iota(jnp.int32, (row_heads, width), 0) // group
    never = jnp.int32(1 << 20)
    token = jnp.where(
        (column < cached) & (lax.rem(column, kinds) == head), column // kinds, never
    )
    places = [
        jnp.where(column == cached + i * kinds + head, -1, token) for i in range(batch)
    ]
    for copy in copies[:5]:
        copy.wait()
    fill_tables([own_ref], order, keys_ref, values_ref, heads, page)
    live = live_bias(table_ref, [me * slots + s for s in range(slots)], page, 1)
    bias_ref[...] = live_bias(
        table_ref,
        [owner(me, replicas) * slots + s for owner in owners for s in range(slots)],
        page,
        8,
    )
    keys = keys_ref[...]
    values = values_ref[...]
    block_rows = wave * batch * row_heads
    for turn in range(waves):
        copies[5 + turn].wait()
        rows = pl.ds(turn * block_rows, block_rows)
        q = q_ref[rows]
        q_wide = head_concat(q, heads, group)
        wide_ref[rows] = q_wide
        prefix = contract_last(q_wide, keys) * scale + live
        pieces = []
        scores = []
        for i in range(wave * batch):
            request = turn * wave * batch + i
            kv = jnp.concatenate(
                [
                    suffix_ref[request * cached : (request + 1) * cached],
                    new_ref[request // batch * fresh : (request // batch + 1) * fresh],
                ],
                axis=0,
            )
            pieces.append(kv)
            score = contract_last(q[i * row_heads : (i + 1) * row_heads], kv) * scale
            scores.append(
                jnp.where(places[i % batch] < lens_ref[request], score, masked_score)
            )
        score = jnp.concatenate(scores, axis=0)
        row_max = jnp.max(jnp.maximum(prefix, score), axis=1, keepdims=True)
        weights = jnp.exp2(score - row_max)
        prefix_weights = jnp.exp2(prefix - row_max)
        part_ref[rows] = weights + prefix_weights
        max_ref[rows] = jnp.broadcast_to(row_max, weights.shape)
        rounded = pltpu.roll(weights, heads, 1).astype(jnp.bfloat16)
        wide = jnp.dot(
            prefix_weights.astype(jnp.bfloat16), values, preferred_element_type=jnp.float32
        )
        attended = [
            jnp.dot(
                rounded[i * row_heads : (i + 1) * row_heads],
                pieces[i],
                preferred_element_type=jnp.float32,
            )
            for i in range(wave * batch)
        ]
        acc_ref[rows] = jnp.concatenate(attended, axis=0) + head_select(wide, heads, group)


def absorb(sizes, rows, wide_ref, acc_ref, max_ref, part_ref, keys, values, live):
    heads, group, scale = sizes
    score = contract_last(wide_ref[rows], keys) * scale + live
    chunks = [score[:, i : i + lanes] for i in range(0, score.shape[1], lanes)]
    top = functools.reduce(jnp.maximum, chunks)
    earlier = max_ref[rows]
    row_max = jnp.maximum(earlier, jnp.max(top, axis=1, keepdims=True))
    weights = [jnp.exp2(chunk - row_max) for chunk in chunks]
    factor = jnp.exp2(earlier - row_max)
    part = part_ref[rows] * factor + functools.reduce(jnp.add, weights)
    rounded = jnp.concatenate([w.astype(jnp.bfloat16) for w in weights], axis=1)
    wide = jnp.dot(rounded, values, preferred_element_type=jnp.float32)
    return acc_ref[rows] * factor + head_select(wide, heads, group), row_max, part


def fold_body(sizes, place, *refs):
    heads, group, page, scale, block_rows, replicas = sizes
    count_in, wide_ref, acc_in, max_in, part_in, bias_ref = refs[:6]
    raws = refs[6:-6]
    count_ref, acc_ref, max_ref, part_ref, keys_ref, values_ref = refs[-6:]
    count_ref[...] = jnp.broadcast_to(count_in[:1, :1], count_ref.shape)
    kinds = 2 * heads
    fill_tables(raws, page_order(page * kinds, kinds), keys_ref, values_ref, heads, page)
    keys = keys_ref[...]
    values = values_ref[...]
    live = bias_ref[:1, place : place + keys.shape[0]]
    for start in range(0, wide_ref.shape[0], block_rows):
        rows = pl.ds(start, block_rows)
        acc_ref[rows], max_ref[rows], part_ref[rows] = absorb(
            (heads, group, scale), rows, wide_ref, acc_in, max_in, part_in, keys, values, live
        )


def finish_body(sizes, place, *refs):
    heads, group, page, scale, block_rows, replicas = sizes
    count_ref, wide_ref, acc_in, max_in, part_in, bias_ref = refs[:6]
    raws = refs[6:-5]
    out_hbm, out_ref, keys_ref, values_ref, sem = refs[-5:]
    kinds = 2 * heads
    fill_tables(raws, page_order(page * kinds, kinds), keys_ref, values_ref, heads, page)
    keys = keys_ref[...]
    values = values_ref[...]
    live = bias_ref[:1, place : place + keys.shape[0]]
    live_rows = count_ref[:1, :] * (heads * group)
    for start in range(0, wide_ref.shape[0], block_rows):
        rows = pl.ds(start, block_rows)
        acc, row_max, part = absorb(
            (heads, group, scale), rows, wide_ref, acc_in, max_in, part_in, keys, values, live
        )
        total = jnp.broadcast_to(jnp.sum(part, axis=1, keepdims=True), part.shape)
        row = start + lax.broadcasted_iota(jnp.int32, part.shape, 0)
        share = jnp.where(row < live_rows, 1.0 / total, 0.0)
        out_ref[rows] = (acc * share).astype(jnp.bfloat16)
    copy = pltpu.make_async_copy(out_ref, out_hbm, sem)
    copy.start()
    copy.wait()


def vmem():
    return pl.BlockSpec(memory_space=pltpu.VMEM)


def hbm():
    return pl.BlockSpec(memory_space=pltpu.HBM)


def xor_exchange(values, step):
    return lax.ppermute(values, "replica", [(i, i ^ step) for i in range(4)])


def doubling_start(raw):
    owners = [lambda me, n, step=step: jnp.bitwise_xor(me, step) for step in (3, 1, 2)]
    return xor_exchange(raw, 3), xor_exchange(raw, 1), owners


def doubling_finish(across, near, anchor):
    across, anchor = lax.optimization_barrier((across, anchor))
    return [[across, near], [xor_exchange(across, 1)]], anchor


def gathered_stages(raw, replicas):
    everything = lax.all_gather(raw, "replica", axis=0, tiled=True)
    owners = [lambda me, n, at=at: jnp.where(me == at, -1, at) for at in range(replicas)]
    together = math.gcd(replicas, 4) * raw.shape[0]
    return [
        [everything[i : i + together]] for i in range(0, everything.shape[0], together)
    ], owners


def shards(replicas, queries, prefix_pool, page_table, suffix_kv, new_kv, suffix_len, counts):
    requests, head_count, width = queries.shape
    slots, page, unused, heads, width = prefix_pool.shape
    suffix = suffix_kv.shape[1]
    group = head_count // heads
    kinds = 2 * heads
    scale = width**-0.5 * math.log2(math.e)
    raw = prefix_pool.reshape(slots * page * kinds, width)
    batch = (-suffix * kinds) % lanes // kinds
    wave = requests // batch
    block_rows = 256
    rows = requests * head_count
    block_tokens = slots * page
    doubling = replicas == 4
    if doubling:
        across, near, owners = doubling_start(raw)
    else:
        stages, owners = gathered_stages(raw, replicas)
    suffix_rows = requests * suffix * kinds
    full = jax.ShapeDtypeStruct((rows, lanes), jnp.float32)
    params = pltpu.CompilerParams(vmem_limit_bytes=24 << 20)

    def cost(tokens):
        return pl.CostEstimate(
            flops=4 * rows * tokens * width, bytes_accessed=3 << 20, transcendentals=rows * tokens
        )

    def tables(tokens):
        return [pltpu.VMEM((tokens, heads * width), jnp.bfloat16)] * 2

    acc, row_max, part, q_wide, bias = pl.pallas_call(
        functools.partial(
            local_body, (heads, group, page, suffix, scale, batch, replicas, wave), owners
        ),
        out_shape=[
            full,
            full,
            full,
            jax.ShapeDtypeStruct((rows, heads * width), jnp.bfloat16),
            jax.ShapeDtypeStruct((8, len(owners) * block_tokens), jnp.float32),
        ],
        in_specs=[hbm()] * 6,
        out_specs=[vmem()] * 5,
        scratch_shapes=[
            pltpu.SMEM(page_table.shape, jnp.int32),
            pltpu.SMEM(suffix_len.shape, jnp.int32),
            pltpu.VMEM((rows, width), jnp.bfloat16),
            pltpu.VMEM(raw.shape, jnp.bfloat16),
            pltpu.VMEM((suffix_rows, width), jnp.bfloat16),
            pltpu.VMEM((requests * kinds, width), jnp.bfloat16),
            *tables(block_tokens),
            pltpu.SemaphoreType.DMA((5 + requests // batch // wave,)),
        ],
        compiler_params=params,
        cost_estimate=cost(2 * block_tokens),
        name="local_part",
    )(
        *[
            pltpu.with_memory_space_constraint(value, pltpu.HBM)
            for value in (
                page_table,
                suffix_len,
                queries.reshape(rows, width),
                raw,
                suffix_kv.reshape(suffix_rows, width),
                new_kv.reshape(requests * kinds, width),
            )
        ]
    )
    if doubling:
        stages, acc = doubling_finish(across, near, acc)
    sizes = (heads, group, page, scale, block_rows, replicas)
    place = 0
    count = jnp.broadcast_to(counts, (8, lanes)) if len(stages) == 1 else counts.reshape(1, 1)
    for blocks in stages[:-1]:
        tokens = sum(block.shape[0] for block in blocks) // kinds
        count, acc, row_max, part = pl.pallas_call(
            functools.partial(fold_body, sizes, place),
            out_shape=[jax.ShapeDtypeStruct((8, lanes), jnp.int32)] + [full] * 3,
            in_specs=[vmem()] * (6 + len(blocks)),
            out_specs=[vmem()] * 4,
            scratch_shapes=tables(tokens),
            compiler_params=params,
            cost_estimate=cost(tokens),
            name="fold_part",
        )(count, q_wide, acc, row_max, part, bias, *blocks)
        place += tokens
    tokens = sum(block.shape[0] for block in stages[-1]) // kinds
    out = pl.pallas_call(
        functools.partial(finish_body, sizes, place),
        out_shape=jax.ShapeDtypeStruct((rows, width), jnp.bfloat16),
        in_specs=[vmem()] * (6 + len(stages[-1])),
        out_specs=hbm(),
        scratch_shapes=[
            pltpu.VMEM((rows, width), jnp.bfloat16),
            *tables(tokens),
            pltpu.SemaphoreType.DMA,
        ],
        compiler_params=params,
        cost_estimate=cost(tokens),
        name="finish_part",
    )(count, q_wide, acc, row_max, part, bias, *stages[-1])
    return out.reshape(requests, head_count, width)


def solution(mesh):
    placed = (
        P(("groups", "replica"), "tensor", None),
        P(("groups", "replica"), None, None, "tensor", None),
        P("groups"),
        P(("groups", "replica"), None, None, "tensor", None),
        P(("groups", "replica"), None, "tensor", None),
        P(("groups", "replica")),
        P(("groups", "replica")),
    )
    return jax.shard_map(
        functools.partial(shards, mesh.shape["replica"]),
        mesh=mesh,
        in_specs=placed,
        out_specs=P(("groups", "replica"), "tensor", None),
        check_vma=False,
    )
```

profile of v0, /device:TPU:0, one launch (start us, length us, event | category | flops | bytes accessed | tf_op | source)
XLA Modules:
  0.0 16.1 jit_solution(13798953948399803062)
XLA Ops:
  0.0 5.0 %collective-permute-start = (bf16[512,128]{1,0:T(8,128)(2,1)}, bf16[512,128]{1,0:T(8,128)(2,1)S(1)}, u32[]{:S(2)}, u32[]{:S(2)}) collective-permute-start(bf16[512,128]{1,0:T(8,128)(2,1)} %bitcast.9), channel_id=1, source_target_pairs={{0,12},{4,8},{8,4},{12,0},{1,13},{5,9},{9,5},{13,1},{2,14},{6,10},... | collective-permute-start | bytes 393224 | tf_op jit(solution)/shard_map/ppermute | solution.py:253
  5.0 0.0 collective-permute-start.1
  5.1 3.7 %local_part.1 = (f32[1024,128]{1,0:T(8,128)S(1)}, f32[1024,128]{1,0:T(8,128)S(1)}, f32[1024,128]{1,0:T(8,128)S(1)}, bf16[1024,256]{1,0:T(8,128)(2,1)S(1)}, f32[8,384]{1,0:T(8,128)S(1)}) custom-call(s32[6]{0:T(128)} %refs_0_.1, s32[64]{0:T(128)} %refs_1_.1, bf16[1024,128]{1,0:T(8,128)(2,1)} %bitcast.8, bf16[512,128]{1,0:T(8,128)(2,1)} %bitcast.11, ...), custom_call_target="tpu_custom_call" | custom-call | flops 134217728 | bytes 3145728 | tf_op jit(solution)/shard_map/local_part/pallas_call | solution.py:305
  8.7 0.9 %collective-permute-done.refs_6_ = bf16[512,128]{1,0:T(8,128)(2,1)S(1)} collective-permute-done((bf16[512,128]{1,0:T(8,128)(2,1)}, bf16[512,128]{1,0:T(8,128)(2,1)S(1)}, u32[]{:S(2)}, u32[]{:S(2)}) %collective-permute-start) | collective-permute-done | bytes 131104 | tf_op jit(solution)/shard_map/ppermute | solution.py:253
  9.6 1.6 %collective-permute-start.2 = (bf16[512,128]{1,0:T(8,128)(2,1)S(1)}, bf16[512,128]{1,0:T(8,128)(2,1)S(1)}, u32[]{:S(2)}, u32[]{:S(2)}) collective-permute-start(bf16[512,128]{1,0:T(8,128)(2,1)S(1)} %collective-permute-done.refs_6_), channel_id=1, source_target_pairs={{0,4},{4,0},{8,12},{12,8},{1,5},{5,1},{9,13},{13,9},{2,6},{6,2},{1... | collective-permute-start | bytes 393224 | tf_op jit(solution)/shard_map/ppermute | solution.py:253
  11.9 0.1 collective-permute-done.1.refs_7_
  12.0 0.9 %fold_part.1 = (s32[8,128]{1,0:T(8,128)S(1)}, f32[1024,128]{1,0:T(8,128)S(1)}, f32[1024,128]{1,0:T(8,128)S(1)}, f32[1024,128]{1,0:T(8,128)S(1)}) custom-call(s32[1,1]{1,0:T(1,128)} %bitcast.6.refs_0_, bf16[1024,256]{1,0:T(8,128)(2,1)S(1)} %get-tuple-element.16.refs_1_, f32[1024,128]{1,0:T(8,128)S(1)} %get-tuple-element.18.refs_2_, ...), custom_call_target="tpu_custom_call" | custom-call | flops 134217728 | bytes 3145728 | tf_op jit(solution)/shard_map/fold_part/pallas_call | solution.py:351
  12.9 1.7 %collective-permute-done.2.refs_6_ = bf16[512,128]{1,0:T(8,128)(2,1)S(1)} collective-permute-done((bf16[512,128]{1,0:T(8,128)(2,1)S(1)}, bf16[512,128]{1,0:T(8,128)(2,1)S(1)}, u32[]{:S(2)}, u32[]{:S(2)}) %collective-permute-start.2) | collective-permute-done | bytes 131104 | tf_op jit(solution)/shard_map/ppermute | solution.py:253
  14.6 1.5 %finish_part.1 = bf16[1024,128]{1,0:T(8,128)(2,1)} custom-call(s32[8,128]{1,0:T(8,128)S(1)} %get-tuple-element.23.refs_0_, bf16[1024,256]{1,0:T(8,128)(2,1)S(1)} %get-tuple-element.16.refs_1_, f32[1024,128]{1,0:T(8,128)S(1)} %get-tuple-element.24.refs_2_, f32[1024,128]{1,0:T(8,128)S(1)} %get-tuple-element.25.refs_3_, ...), custom_call_target="tpu_custom_call" | custom-call | flops 67108864 | bytes 3145728 | tf_op jit(solution)/shard_map/finish_part/pallas_call | solution.py:363
Async XLA Ops:
  0.0 9.6 %collective-permute-start = (bf16[512,128]{1,0:T(8,128)(2,1)}, bf16[512,128]{1,0:T(8,128)(2,1)S(1)}, u32[]{:S(2)}, u32[]{:S(2)}) collective-permute-start(bf16[512,128]{1,0:T(8,128)(2,1)} %bitcast.9), channel_id=1, source_target_pairs={{0,12},{4,8},{8,4},{12,0},{1,13},{5,9},{9,5},{13,1},{2,14},{6,10},... | collective-permute-start | bytes 393224 | tf_op jit(solution)/shard_map/ppermute | solution.py:253
  5.0 6.9 %collective-permute-start.1 = (bf16[512,128]{1,0:T(8,128)(2,1)}, bf16[512,128]{1,0:T(8,128)(2,1)S(1)}, u32[]{:S(2)}, u32[]{:S(2)}) collective-permute-start(bf16[512,128]{1,0:T(8,128)(2,1)} %bitcast.10), channel_id=1, source_target_pairs={{0,4},{4,0},{8,12},{12,8},{1,5},{5,1},{9,13},{13,9},{2,6},{6,2},{1... | collective-permute-start | bytes 393224 | tf_op jit(solution)/shard_map/ppermute | solution.py:253
  9.6 5.0 %collective-permute-start.2 = (bf16[512,128]{1,0:T(8,128)(2,1)S(1)}, bf16[512,128]{1,0:T(8,128)(2,1)S(1)}, u32[]{:S(2)}, u32[]{:S(2)}) collective-permute-start(bf16[512,128]{1,0:T(8,128)(2,1)S(1)} %collective-permute-done.refs_6_), channel_id=1, source_target_pairs={{0,4},{4,0},{8,12},{12,8},{1,5},{5,1},{9,13},{13,9},{2,6},{6,2},{1... | collective-permute-start | bytes 393224 | tf_op jit(solution)/shard_map/ppermute | solution.py:253
where the time goes:
time: 16.3 us; the launch traced here: 16.1 us
  starting transfers between devices  6.7 us (41%)
  Pallas kernels  6.1 us (37%)
  waiting for transfers between devices  2.64 us (16%)
  between operations  0.67 us (4%)
    ppermute x3, starting transfers between devices, xor_exchange(): return lax.ppermute(values, 'replica', [(i, i ^ step) for i in range(4)])  6.7 us
    pallas_call x1, Pallas kernels, shards(): pl.pallas_call(functools.partial(local_body, (heads, group, page, suffix,...  3.68 us
    ppermute x3, waiting for transfers between devices, xor_exchange(): return lax.ppermute(values, 'replica', [(i, i ^ step) for i in range(4)])  2.64 us
    pallas_call x1, Pallas kernels, shards(): pl.pallas_call(functools.partial(finish_body, sizes, place), out_shape=ja...  1.51 us
    pallas_call x1, Pallas kernels, shards(): pl.pallas_call(functools.partial(fold_body, sizes, place), out_shape=[jax...  0.91 us
  transfers between devices with their start and end apart: 3, of which 3 were waited for; matrix products, arithmetic and copies ran while one was open for 0% of the time, Pallas kernels for 28%

commit v1 on v0

--- a/solution.py
+++ b/solution.py
@@ -84,12 +84,14 @@
     return lax.dot_general(a, b, (((1,), (1,)), ((), ())), preferred_element_type=jnp.float32)
 
 
-def local_body(sizes, owners, *refs):
+def local_body(sizes, early_owners, owners, *refs):
     heads, group, page, suffix, scale, batch, replicas, wave = sizes
     table_hbm, lens_hbm, q_hbm, own_hbm, suffix_hbm, new_hbm = refs[:6]
-    acc_ref, max_ref, part_ref, wide_ref, bias_ref = refs[6:11]
-    table_ref, lens_ref, q_ref, own_ref, suffix_ref, new_ref = refs[11:17]
-    keys_ref, values_ref, sems = refs[17:]
+    early = refs[6 : 6 + len(early_owners)]
+    refs = refs[6 + len(early_owners) :]
+    acc_ref, max_ref, part_ref, wide_ref, bias_ref = refs[:5]
+    table_ref, lens_ref, q_ref, own_ref, suffix_ref, new_ref = refs[5:11]
+    keys_ref, values_ref, sems = refs[11:]
     kinds = 2 * heads
     row_heads = heads * group
     cached = suffix * kinds
@@ -128,8 +130,11 @@
     ]
     for copy in copies[:5]:
         copy.wait()
-    fill_tables([own_ref], order, keys_ref, values_ref, heads, page)
-    live = live_bias(table_ref, [me * slots + s for s in range(slots)], page, 1)
+    fill_tables([own_ref, *early], order, keys_ref, values_ref, heads, page)
+    near = [me] + [owner(me, replicas) for owner in early_owners]
+    live = live_bias(
+        table_ref, [owner * slots + s for owner in near for s in range(slots)], page, 1
+    )
     bias_ref[...] = live_bias(
         table_ref,
         [owner(me, replicas) * slots + s for owner in owners for s in range(slots)],
@@ -163,14 +168,18 @@
                 jnp.where(places[i % batch] < lens_ref[request], score, masked_score)
             )
         score = jnp.concatenate(scores, axis=0)
-        row_max = jnp.max(jnp.maximum(prefix, score), axis=1, keepdims=True)
+        chunks = [prefix[:, i : i + lanes] for i in range(0, prefix.shape[1], lanes)]
+        top = functools.reduce(jnp.maximum, chunks, score)
+        row_max = jnp.max(top, axis=1, keepdims=True)
         weights = jnp.exp2(score - row_max)
-        prefix_weights = jnp.exp2(prefix - row_max)
-        part_ref[rows] = weights + prefix_weights
+        prefix_weights = [jnp.exp2(chunk - row_max) for chunk in chunks]
+        part_ref[rows] = functools.reduce(jnp.add, prefix_weights, weights)
         max_ref[rows] = jnp.broadcast_to(row_max, weights.shape)
         rounded = pltpu.roll(weights, heads, 1).astype(jnp.bfloat16)
         wide = jnp.dot(
-            prefix_weights.astype(jnp.bfloat16), values, preferred_element_type=jnp.float32
+            jnp.concatenate([w.astype(jnp.bfloat16) for w in prefix_weights], axis=1),
+            values,
+            preferred_element_type=jnp.float32,
         )
         attended = [
             jnp.dot(
@@ -216,12 +225,14 @@
         )
 
 
-def finish_body(sizes, place, *refs):
+def finish_body(sizes, place, choices, *refs):
     heads, group, page, scale, block_rows, replicas = sizes
     count_ref, wide_ref, acc_in, max_in, part_in, bias_ref = refs[:6]
     raws = refs[6:-5]
     out_hbm, out_ref, keys_ref, values_ref, sem = refs[-5:]
     kinds = 2 * heads
+    me = lax.axis_index("replica")
+    raws = [choice(me, raws) for choice in choices]
     fill_tables(raws, page_order(page * kinds, kinds), keys_ref, values_ref, heads, page)
     keys = keys_ref[...]
     values = values_ref[...]
@@ -253,14 +264,26 @@
     return lax.ppermute(values, "replica", [(i, i ^ step) for i in range(4)])
 
 
-def doubling_start(raw):
-    owners = [lambda me, n, step=step: jnp.bitwise_xor(me, step) for step in (3, 1, 2)]
-    return xor_exchange(raw, 3), xor_exchange(raw, 1), owners
-
-
-def doubling_finish(across, near, anchor):
-    across, anchor = lax.optimization_barrier((across, anchor))
-    return [[across, near], [xor_exchange(across, 1)]], anchor
+def line_plan(raw):
+    def exchange(values, partners):
+        return lax.ppermute(values, "replica", list(enumerate(partners)))
+
+    middle = exchange(raw, (0, 2, 1, 3))
+    near = exchange(raw, (1, 0, 3, 2))
+    ends = exchange(raw, (3, 1, 2, 0))
+    outward = exchange(middle, (1, 0, 3, 2))
+    across = exchange(near, (0, 2, 1, 3))
+    late = [middle, ends, across, outward]
+
+    def pick(first):
+        def choice(me, blocks):
+            inner = (me == 1) | (me == 2)
+            return lax.select(inner, blocks[first][...], blocks[first + 1][...])
+
+        return choice
+
+    owners = [lambda me, n, step=step: jnp.bitwise_xor(me, step) for step in (1, 3, 2)]
+    return [near], owners[:1], late, owners[1:], [pick(0), pick(2)]
 
 
 def gathered_stages(raw, replicas):
@@ -285,9 +308,10 @@
     block_rows = 256
     rows = requests * head_count
     block_tokens = slots * page
-    doubling = replicas == 4
-    if doubling:
-        across, near, owners = doubling_start(raw)
+    early, early_owners, choices = [], [], None
+    if replicas == 4:
+        early, early_owners, late, owners, choices = line_plan(raw)
+        stages = [late]
     else:
         stages, owners = gathered_stages(raw, replicas)
     suffix_rows = requests * suffix * kinds
@@ -304,7 +328,10 @@
 
     acc, row_max, part, q_wide, bias = pl.pallas_call(
         functools.partial(
-            local_body, (heads, group, page, suffix, scale, batch, replicas, wave), owners
+            local_body,
+            (heads, group, page, suffix, scale, batch, replicas, wave),
+            early_owners,
+            owners,
         ),
         out_shape=[
             full,
@@ -313,7 +340,7 @@
             jax.ShapeDtypeStruct((rows, heads * width), jnp.bfloat16),
             jax.ShapeDtypeStruct((8, len(owners) * block_tokens), jnp.float32),
         ],
-        in_specs=[hbm()] * 6,
+        in_specs=[hbm()] * 6 + [vmem()] * len(early),
         out_specs=[vmem()] * 5,
         scratch_shapes=[
             pltpu.SMEM(page_table.shape, jnp.int32),
@@ -322,7 +349,7 @@
             pltpu.VMEM(raw.shape, jnp.bfloat16),
             pltpu.VMEM((suffix_rows, width), jnp.bfloat16),
             pltpu.VMEM((requests * kinds, width), jnp.bfloat16),
-            *tables(block_tokens),
+            *tables((1 + len(early)) * block_tokens),
             pltpu.SemaphoreType.DMA((5 + requests // batch // wave,)),
         ],
         compiler_params=params,
@@ -339,10 +366,9 @@
                 suffix_kv.reshape(suffix_rows, width),
                 new_kv.reshape(requests * kinds, width),
             )
-        ]
-    )
-    if doubling:
-        stages, acc = doubling_finish(across, near, acc)
+        ],
+        *early,
+    )
     sizes = (heads, group, page, scale, block_rows, replicas)
     place = 0
     count = jnp.broadcast_to(counts, (8, lanes)) if len(stages) == 1 else counts.reshape(1, 1)
@@ -359,9 +385,11 @@
             name="fold_part",
         )(count, q_wide, acc, row_max, part, bias, *blocks)
         place += tokens
-    tokens = sum(block.shape[0] for block in stages[-1]) // kinds
+    if choices is None:
+        choices = [lambda me, blocks, i=i: blocks[i] for i in range(len(stages[-1]))]
+    tokens = len(choices) * stages[-1][0].shape[0] // kinds
     out = pl.pallas_call(
-        functools.partial(finish_body, sizes, place),
+        functools.partial(finish_body, sizes, place, choices),
         out_shape=jax.ShapeDtypeStruct((rows, width), jnp.bfloat16),
         in_specs=[vmem()] * (6 + len(stages[-1])),
         out_specs=hbm(),

time: 16.3 us -> 19 us (1.17)
  starting transfers between devices: 6.7 us -> 11 us
  waiting for transfers between devices: 2.64 us -> 1.7 us
  Pallas kernels: 6.1 us -> 5.4 us
    ppermute x3 -> x5, starting transfers between devices: 6.7 us -> 11 us  [exchange(): return lax.ppermute(values, 'replica', list(enumerate(partners)))]
    ppermute x3 -> x5, waiting for transfers between devices: 2.64 us -> 1.7 us  [exchange(): return lax.ppermute(values, 'replica', list(enumerate(partners)))]
    pallas_call x2 -> x1, Pallas kernels: 2.42 us -> 1.66 us  [shards(): pl.pallas_call(functools.partial(finish_body, sizes, place, choices), out...]
  transfers between devices with their start and end apart: 3 -> 5, of which waited for: 3 -> 2; matrix products, arithmetic and copies ran while one was open for 0% -> 0% of each run, Pallas kernels for 28% -> 20%
where the time goes in v1:
time: 19 us; the launch traced here: 18.8 us
  starting transfers between devices  11 us (58%)
  Pallas kernels  5.4 us (28%)
  waiting for transfers between devices  1.7 us (9%)
  between operations  0.68 us (4%)
    ppermute x5, starting transfers between devices, exchange(): return lax.ppermute(values, 'replica', list(enumerate(partners)))  11 us
    pallas_call x1, Pallas kernels, shards(): pl.pallas_call(functools.partial(local_body, (heads, group, page, suffix,...  3.74 us
    ppermute x5, waiting for transfers between devices, exchange(): return lax.ppermute(values, 'replica', list(enumerate(partners)))  1.7 us
    pallas_call x1, Pallas kernels, shards(): pl.pallas_call(functools.partial(finish_body, sizes, place, choices), out...  1.66 us
  transfers between devices with their start and end apart: 5, of which 2 were waited for; matrix products, arithmetic and copies ran while one was open for 0% of the time, Pallas kernels for 20%

profile of v1, /device:TPU:0, one launch (start us, length us, event | category | flops | bytes accessed | tf_op | source)
XLA Modules:
  0.0 18.8 jit_solution(10781568295216956745)
XLA Ops:
  0.0 1.6 %collective-permute-start.1 = (bf16[512,128]{1,0:T(8,128)(2,1)}, bf16[512,128]{1,0:T(8,128)(2,1)S(1)}, u32[]{:S(2)}, u32[]{:S(2)}) collective-permute-start(bf16[512,128]{1,0:T(8,128)(2,1)} %bitcast.9), channel_id=1, source_target_pairs={{0,0},{4,8},{8,4},{12,12},{1,1},{5,9},{9,5},{13,13},{2,2},{6,10},{... | collective-permute-start | bytes 393224 | tf_op jit(solution)/shard_map/ppermute | solution.py:269
  1.6 5.0 %collective-permute-start = (bf16[512,128]{1,0:T(8,128)(2,1)}, bf16[512,128]{1,0:T(8,128)(2,1)S(1)}, u32[]{:S(2)}, u32[]{:S(2)}) collective-permute-start(bf16[512,128]{1,0:T(8,128)(2,1)} %bitcast.10), channel_id=1, source_target_pairs={{0,4},{4,0},{8,12},{12,8},{1,5},{5,1},{9,13},{13,9},{2,6},{6,2},{1... | collective-permute-start | bytes 393224 | tf_op jit(solution)/shard_map/ppermute | solution.py:269
  6.6 3.2 %collective-permute-start.2 = (bf16[512,128]{1,0:T(8,128)(2,1)}, bf16[512,128]{1,0:T(8,128)(2,1)S(1)}, u32[]{:S(2)}, u32[]{:S(2)}) collective-permute-start(bf16[512,128]{1,0:T(8,128)(2,1)} %bitcast.11), channel_id=1, source_target_pairs={{0,12},{4,4},{8,8},{12,0},{1,13},{5,5},{9,9},{13,1},{2,14},{6,6},{... | collective-permute-start | bytes 393224 | tf_op jit(solution)/shard_map/ppermute | solution.py:269
  9.8 0.0 collective-permute-done.1.refs_6_
  9.8 0.5 %collective-permute-start.4 = (bf16[512,128]{1,0:T(8,128)(2,1)S(1)}, bf16[512,128]{1,0:T(8,128)(2,1)S(1)}, u32[]{:S(2)}, u32[]{:S(2)}) collective-permute-start(bf16[512,128]{1,0:T(8,128)(2,1)S(1)} %collective-permute-done.1.refs_6_), channel_id=1, source_target_pairs={{0,4},{4,0},{8,12},{12,8},{1,5},{5,1},{9,13},{13,9},{2,6},{6,2},{1... | collective-permute-start | bytes 393224 | tf_op jit(solution)/shard_map/ppermute | solution.py:269
  10.4 0.0 collective-permute-done.refs_6_
  10.4 0.7 %collective-permute-start.3 = (bf16[512,128]{1,0:T(8,128)(2,1)S(1)}, bf16[512,128]{1,0:T(8,128)(2,1)S(1)}, u32[]{:S(2)}, u32[]{:S(2)}) collective-permute-start(bf16[512,128]{1,0:T(8,128)(2,1)S(1)} %collective-permute-done.refs_6_), channel_id=1, source_target_pairs={{0,0},{4,8},{8,4},{12,12},{1,1},{5,9},{9,5},{13,13},{2,2},{6,10},{... | collective-permute-start | bytes 393224 | tf_op jit(solution)/shard_map/ppermute | solution.py:269
  11.7 3.7 %local_part.1 = (f32[1024,128]{1,0:T(8,128)S(1)}, f32[1024,128]{1,0:T(8,128)S(1)}, f32[1024,128]{1,0:T(8,128)S(1)}, bf16[1024,256]{1,0:T(8,128)(2,1)S(1)}, f32[8,256]{1,0:T(8,128)S(1)}) custom-call(s32[6]{0:T(128)} %refs_0_.1, s32[64]{0:T(128)} %refs_1_.1, bf16[1024,128]{1,0:T(8,128)(2,1)} %bitcast.8, bf16[512,128]{1,0:T(8,128)(2,1)} %bitcast.12, ...), custom_call_target="tpu_custom_call" | custom-call | flops 134217728 | bytes 3145728 | tf_op jit(solution)/shard_map/local_part/pallas_call | solution.py:329
  15.4 1.3 %collective-permute-done.2.refs_7_ = bf16[512,128]{1,0:T(8,128)(2,1)S(1)} collective-permute-done((bf16[512,128]{1,0:T(8,128)(2,1)}, bf16[512,128]{1,0:T(8,128)(2,1)S(1)}, u32[]{:S(2)}, u32[]{:S(2)}) %collective-permute-start.2) | collective-permute-done | bytes 131104 | tf_op jit(solution)/shard_map/ppermute | solution.py:269
  16.7 0.4 %collective-permute-done.4.refs_9_ = bf16[512,128]{1,0:T(8,128)(2,1)S(1)} collective-permute-done((bf16[512,128]{1,0:T(8,128)(2,1)S(1)}, bf16[512,128]{1,0:T(8,128)(2,1)S(1)}, u32[]{:S(2)}, u32[]{:S(2)}) %collective-permute-start.4) | collective-permute-done | bytes 131104 | tf_op jit(solution)/shard_map/ppermute | solution.py:269
  17.1 0.0 collective-permute-done.3.refs_8_
  17.1 1.7 %finish_part.1 = bf16[1024,128]{1,0:T(8,128)(2,1)} custom-call(s32[8,128]{1,0:T(8,128)S(1)} %broadcast_in_dim.2.refs_0_, bf16[1024,256]{1,0:T(8,128)(2,1)S(1)} %get-tuple-element.10.refs_1_, f32[1024,128]{1,0:T(8,128)S(1)} %get-tuple-element.11.refs_2_, f32[1024,128]{1,0:T(8,128)S(1)} %get-tuple-element.12.refs_3_, ...), custom_call_target="tpu_custom_call" | custom-call | flops 134217728 | bytes 3145728 | tf_op jit(solution)/shard_map/finish_part/pallas_call | solution.py:391
  (1 shorter events, 0.0 us)
Async XLA Ops:
  0.0 9.8 %collective-permute-start.1 = (bf16[512,128]{1,0:T(8,128)(2,1)}, bf16[512,128]{1,0:T(8,128)(2,1)S(1)}, u32[]{:S(2)}, u32[]{:S(2)}) collective-permute-start(bf16[512,128]{1,0:T(8,128)(2,1)} %bitcast.9), channel_id=1, source_target_pairs={{0,0},{4,8},{8,4},{12,12},{1,1},{5,9},{9,5},{13,13},{2,2},{6,10},{... | collective-permute-start | bytes 393224 | tf_op jit(solution)/shard_map/ppermute | solution.py:269
  1.6 8.8 %collective-permute-start = (bf16[512,128]{1,0:T(8,128)(2,1)}, bf16[512,128]{1,0:T(8,128)(2,1)S(1)}, u32[]{:S(2)}, u32[]{:S(2)}) collective-permute-start(bf16[512,128]{1,0:T(8,128)(2,1)} %bitcast.10), channel_id=1, source_target_pairs={{0,4},{4,0},{8,12},{12,8},{1,5},{5,1},{9,13},{13,9},{2,6},{6,2},{1... | collective-permute-start | bytes 393224 | tf_op jit(solution)/shard_map/ppermute | solution.py:269
  6.6 10.1 %collective-permute-start.2 = (bf16[512,128]{1,0:T(8,128)(2,1)}, bf16[512,128]{1,0:T(8,128)(2,1)S(1)}, u32[]{:S(2)}, u32[]{:S(2)}) collective-permute-start(bf16[512,128]{1,0:T(8,128)(2,1)} %bitcast.11), channel_id=1, source_target_pairs={{0,12},{4,4},{8,8},{12,0},{1,13},{5,5},{9,9},{13,1},{2,14},{6,6},{... | collective-permute-start | bytes 393224 | tf_op jit(solution)/shard_map/ppermute | solution.py:269
  9.8 7.3 %collective-permute-start.4 = (bf16[512,128]{1,0:T(8,128)(2,1)S(1)}, bf16[512,128]{1,0:T(8,128)(2,1)S(1)}, u32[]{:S(2)}, u32[]{:S(2)}) collective-permute-start(bf16[512,128]{1,0:T(8,128)(2,1)S(1)} %collective-permute-done.1.refs_6_), channel_id=1, source_target_pairs={{0,4},{4,0},{8,12},{12,8},{1,5},{5,1},{9,13},{13,9},{2,6},{6,2},{1... | collective-permute-start | bytes 393224 | tf_op jit(solution)/shard_map/ppermute | solution.py:269
  10.4 6.7 %collective-permute-start.3 = (bf16[512,128]{1,0:T(8,128)(2,1)S(1)}, bf16[512,128]{1,0:T(8,128)(2,1)S(1)}, u32[]{:S(2)}, u32[]{:S(2)}) collective-permute-start(bf16[512,128]{1,0:T(8,128)(2,1)S(1)} %collective-permute-done.refs_6_), channel_id=1, source_target_pairs={{0,0},{4,8},{8,4},{12,12},{1,1},{5,9},{9,5},{13,13},{2,2},{6,10},{... | collective-permute-start | bytes 393224 | tf_op jit(solution)/shard_map/ppermute | solution.py:269

commit v2 on v0

--- a/solution.py
+++ b/solution.py
@@ -249,18 +249,35 @@
     return pl.BlockSpec(memory_space=pltpu.HBM)
 
 
-def xor_exchange(values, step):
-    return lax.ppermute(values, "replica", [(i, i ^ step) for i in range(4)])
-
-
-def doubling_start(raw):
-    owners = [lambda me, n, step=step: jnp.bitwise_xor(me, step) for step in (3, 1, 2)]
-    return xor_exchange(raw, 3), xor_exchange(raw, 1), owners
-
-
-def doubling_finish(across, near, anchor):
-    across, anchor = lax.optimization_barrier((across, anchor))
-    return [[across, near], [xor_exchange(across, 1)]], anchor
+def folded_ring(replicas):
+    return list(range(0, replicas, 2)) + list(range(1, replicas, 2))[::-1]
+
+
+def ring_step(values, ring, step):
+    return lax.ppermute(
+        values, "replica", [(ring[i], ring[(i + step) % len(ring)]) for i in range(len(ring))]
+    )
+
+
+def ring_owner(ring, step):
+    def owner(me, n):
+        found = jnp.int32(ring[-step])
+        for i in range(1, len(ring)):
+            found = jnp.where(me == ring[i], ring[(i - step) % len(ring)], found)
+        return found
+
+    return owner
+
+
+def ring_start(raw, replicas):
+    ring = folded_ring(replicas)
+    owners = [ring_owner(ring, step) for step in (1, -1, 2)]
+    return ring_step(raw, ring, 1), ring_step(raw, ring, -1), owners
+
+
+def ring_finish(ahead, back, replicas, anchor):
+    ahead, anchor = lax.optimization_barrier((ahead, anchor))
+    return [[ahead, back], [ring_step(ahead, folded_ring(replicas), 1)]], anchor
 
 
 def gathered_stages(raw, replicas):
@@ -285,9 +302,9 @@
     block_rows = 256
     rows = requests * head_count
     block_tokens = slots * page
-    doubling = replicas == 4
-    if doubling:
-        across, near, owners = doubling_start(raw)
+    two_ways = replicas == 4
+    if two_ways:
+        ahead, back, owners = ring_start(raw, replicas)
     else:
         stages, owners = gathered_stages(raw, replicas)
     suffix_rows = requests * suffix * kinds
@@ -341,8 +358,8 @@
             )
         ]
     )
-    if doubling:
-        stages, acc = doubling_finish(across, near, acc)
+    if two_ways:
+        stages, acc = ring_finish(ahead, back, replicas, acc)
     sizes = (heads, group, page, scale, block_rows, replicas)
     place = 0
     count = jnp.broadcast_to(counts, (8, lanes)) if len(stages) == 1 else counts.reshape(1, 1)

time: 16.3 us -> 16.1 us (0.988)
  waiting for transfers between devices: 2.64 us -> 1.84 us
  starting transfers between devices: 6.7 us -> 7.31 us
    ppermute x3, waiting for transfers between devices: 2.64 us -> 1.84 us  [ring_step(): lax.ppermute(values, 'replica', [(ring[i], ring[(i + step) % len(ring)])...]
    ppermute x3, starting transfers between devices: 6.7 us -> 7.31 us  [ring_step(): lax.ppermute(values, 'replica', [(ring[i], ring[(i + step) % len(ring)])...]
  transfers between devices with their start and end apart: 3 -> 3, of which waited for: 3 -> 2; matrix products, arithmetic and copies ran while one was open for 0% -> 0% of each run, Pallas kernels for 28% -> 29%
where the time goes in v2:
time: 16.1 us; the launch traced here: 15.9 us
  starting transfers between devices  7.31 us (45%)
  Pallas kernels  6.1 us (38%)
  waiting for transfers between devices  1.84 us (11%)
  between operations  0.68 us (4%)
    ppermute x3, starting transfers between devices, ring_step(): lax.ppermute(values, 'replica', [(ring[i], ring[(i + step) % len(ring)])...  7.31 us
    pallas_call x1, Pallas kernels, shards(): pl.pallas_call(functools.partial(local_body, (heads, group, page, suffix,...  3.68 us
    ppermute x3, waiting for transfers between devices, ring_step(): lax.ppermute(values, 'replica', [(ring[i], ring[(i + step) % len(ring)])...  1.84 us
    pallas_call x1, Pallas kernels, shards(): pl.pallas_call(functools.partial(finish_body, sizes, place), out_shape=ja...  1.51 us
    pallas_call x1, Pallas kernels, shards(): pl.pallas_call(functools.partial(fold_body, sizes, place), out_shape=[jax...  0.91 us
  transfers between devices with their start and end apart: 3, of which 2 were waited for; matrix products, arithmetic and copies ran while one was open for 0% of the time, Pallas kernels for 29%

profile of v2, /device:TPU:0, one launch (start us, length us, event | category | flops | bytes accessed | tf_op | source)
XLA Modules:
  0.0 15.9 jit_solution(17981460887400495970)
XLA Ops:
  0.0 4.0 %collective-permute-start = (bf16[512,128]{1,0:T(8,128)(2,1)}, bf16[512,128]{1,0:T(8,128)(2,1)S(1)}, u32[]{:S(2)}, u32[]{:S(2)}) collective-permute-start(bf16[512,128]{1,0:T(8,128)(2,1)} %bitcast.9), channel_id=1, source_target_pairs={{0,8},{8,12},{12,4},{4,0},{1,9},{9,13},{13,5},{5,1},{2,10},{10,14}... | collective-permute-start | bytes 393224 | tf_op jit(solution)/shard_map/ppermute | solution.py:257
  4.0 0.0 collective-permute-start.1
  4.0 3.7 %local_part.1 = (f32[1024,128]{1,0:T(8,128)S(1)}, f32[1024,128]{1,0:T(8,128)S(1)}, f32[1024,128]{1,0:T(8,128)S(1)}, bf16[1024,256]{1,0:T(8,128)(2,1)S(1)}, f32[8,384]{1,0:T(8,128)S(1)}) custom-call(s32[6]{0:T(128)} %refs_0_.1, s32[64]{0:T(128)} %refs_1_.1, bf16[1024,128]{1,0:T(8,128)(2,1)} %bitcast.8, bf16[512,128]{1,0:T(8,128)(2,1)} %bitcast.11, ...), custom_call_target="tpu_custom_call" | custom-call | flops 134217728 | bytes 3145728 | tf_op jit(solution)/shard_map/local_part/pallas_call | solution.py:322
  7.7 0.5 %collective-permute-done.refs_6_ = bf16[512,128]{1,0:T(8,128)(2,1)S(1)} collective-permute-done((bf16[512,128]{1,0:T(8,128)(2,1)}, bf16[512,128]{1,0:T(8,128)(2,1)S(1)}, u32[]{:S(2)}, u32[]{:S(2)}) %collective-permute-start) | collective-permute-done | bytes 131104 | tf_op jit(solution)/shard_map/ppermute | solution.py:257
  8.3 3.3 %collective-permute-start.2 = (bf16[512,128]{1,0:T(8,128)(2,1)S(1)}, bf16[512,128]{1,0:T(8,128)(2,1)S(1)}, u32[]{:S(2)}, u32[]{:S(2)}) collective-permute-start(bf16[512,128]{1,0:T(8,128)(2,1)S(1)} %collective-permute-done.refs_6_), channel_id=1, source_target_pairs={{0,8},{8,12},{12,4},{4,0},{1,9},{9,13},{13,5},{5,1},{2,10},{10,14}... | collective-permute-start | bytes 393224 | tf_op jit(solution)/shard_map/ppermute | solution.py:257
  12.2 0.0 collective-permute-done.1.refs_7_
  12.2 0.9 %fold_part.1 = (s32[8,128]{1,0:T(8,128)S(1)}, f32[1024,128]{1,0:T(8,128)S(1)}, f32[1024,128]{1,0:T(8,128)S(1)}, f32[1024,128]{1,0:T(8,128)S(1)}) custom-call(s32[1,1]{1,0:T(1,128)} %bitcast.6.refs_0_, bf16[1024,256]{1,0:T(8,128)(2,1)S(1)} %get-tuple-element.16.refs_1_, f32[1024,128]{1,0:T(8,128)S(1)} %get-tuple-element.18.refs_2_, ...), custom_call_target="tpu_custom_call" | custom-call | flops 134217728 | bytes 3145728 | tf_op jit(solution)/shard_map/fold_part/pallas_call | solution.py:368
  13.1 1.3 %collective-permute-done.2.refs_6_ = bf16[512,128]{1,0:T(8,128)(2,1)S(1)} collective-permute-done((bf16[512,128]{1,0:T(8,128)(2,1)S(1)}, bf16[512,128]{1,0:T(8,128)(2,1)S(1)}, u32[]{:S(2)}, u32[]{:S(2)}) %collective-permute-start.2) | collective-permute-done | bytes 131104 | tf_op jit(solution)/shard_map/ppermute | solution.py:257
  14.4 1.5 %finish_part.1 = bf16[1024,128]{1,0:T(8,128)(2,1)} custom-call(s32[8,128]{1,0:T(8,128)S(1)} %get-tuple-element.23.refs_0_, bf16[1024,256]{1,0:T(8,128)(2,1)S(1)} %get-tuple-element.16.refs_1_, f32[1024,128]{1,0:T(8,128)S(1)} %get-tuple-element.24.refs_2_, f32[1024,128]{1,0:T(8,128)S(1)} %get-tuple-element.25.refs_3_, ...), custom_call_target="tpu_custom_call" | custom-call | flops 67108864 | bytes 3145728 | tf_op jit(solution)/shard_map/finish_part/pallas_call | solution.py:380
Async XLA Ops:
  0.0 8.3 %collective-permute-start = (bf16[512,128]{1,0:T(8,128)(2,1)}, bf16[512,128]{1,0:T(8,128)(2,1)S(1)}, u32[]{:S(2)}, u32[]{:S(2)}) collective-permute-start(bf16[512,128]{1,0:T(8,128)(2,1)} %bitcast.9), channel_id=1, source_target_pairs={{0,8},{8,12},{12,4},{4,0},{1,9},{9,13},{13,5},{5,1},{2,10},{10,14}... | collective-permute-start | bytes 393224 | tf_op jit(solution)/shard_map/ppermute | solution.py:257
  4.0 8.1 %collective-permute-start.1 = (bf16[512,128]{1,0:T(8,128)(2,1)}, bf16[512,128]{1,0:T(8,128)(2,1)S(1)}, u32[]{:S(2)}, u32[]{:S(2)}) collective-permute-start(bf16[512,128]{1,0:T(8,128)(2,1)} %bitcast.10), channel_id=1, source_target_pairs={{0,4},{8,0},{12,8},{4,12},{1,5},{9,1},{13,9},{5,13},{2,6},{10,2},{... | collective-permute-start | bytes 393224 | tf_op jit(solution)/shard_map/ppermute | solution.py:257
  8.3 6.2 %collective-permute-start.2 = (bf16[512,128]{1,0:T(8,128)(2,1)S(1)}, bf16[512,128]{1,0:T(8,128)(2,1)S(1)}, u32[]{:S(2)}, u32[]{:S(2)}) collective-permute-start(bf16[512,128]{1,0:T(8,128)(2,1)S(1)} %collective-permute-done.refs_6_), channel_id=1, source_target_pairs={{0,8},{8,12},{12,4},{4,0},{1,9},{9,13},{13,5},{5,1},{2,10},{10,14}... | collective-permute-start | bytes 393224 | tf_op jit(solution)/shard_map/ppermute | solution.py:257

commit v3 on v2

--- a/solution.py
+++ b/solution.py
@@ -84,29 +84,22 @@
     return lax.dot_general(a, b, (((1,), (1,)), ((), ())), preferred_element_type=jnp.float32)
 
 
-def local_body(sizes, owners, *refs):
-    heads, group, page, suffix, scale, batch, replicas, wave = sizes
+def load_body(sizes, owners, *refs):
+    heads, group, page, suffix, batch, replicas = sizes
     table_hbm, lens_hbm, q_hbm, own_hbm, suffix_hbm, new_hbm = refs[:6]
-    acc_ref, max_ref, part_ref, wide_ref, bias_ref = refs[6:11]
-    table_ref, lens_ref, q_ref, own_ref, suffix_ref, new_ref = refs[11:17]
-    keys_ref, values_ref, sems = refs[17:]
+    q_ref, suffix_ref, new_ref, keys_ref, values_ref, wide_ref, mask_ref, bias_ref = refs[6:14]
+    table_ref, lens_ref, own_ref, sems = refs[14:]
     kinds = 2 * heads
     row_heads = heads * group
     cached = suffix * kinds
-    fresh = batch * kinds
-    width = cached + fresh
-    batches = q_ref.shape[0] // (batch * row_heads)
-    waves = batches // wave
-    wave_rows = wave * batch * cached
+    width = cached + batch * kinds
     pairs = [
+        (table_hbm, table_ref),
+        (lens_hbm, lens_ref),
         (own_hbm, own_ref),
         (q_hbm, q_ref),
         (new_hbm, new_ref),
-        (table_hbm, table_ref),
-        (lens_hbm, lens_ref),
-    ] + [
-        (suffix_hbm.at[pl.ds(i * wave_rows, wave_rows)], suffix_ref.at[pl.ds(i * wave_rows, wave_rows)])
-        for i in range(waves)
+        (suffix_hbm, suffix_ref),
     ]
     copies = [
         pltpu.make_async_copy(source, target, sems.at[i])
@@ -126,61 +119,69 @@
     places = [
         jnp.where(column == cached + i * kinds + head, -1, token) for i in range(batch)
     ]
-    for copy in copies[:5]:
+    for copy in copies[:2]:
         copy.wait()
-    fill_tables([own_ref], order, keys_ref, values_ref, heads, page)
-    live = live_bias(table_ref, [me * slots + s for s in range(slots)], page, 1)
+    owners = [lambda me, n: me] + owners
     bias_ref[...] = live_bias(
         table_ref,
         [owner(me, replicas) * slots + s for owner in owners for s in range(slots)],
         page,
         8,
     )
-    keys = keys_ref[...]
-    values = values_ref[...]
-    block_rows = wave * batch * row_heads
-    for turn in range(waves):
-        copies[5 + turn].wait()
-        rows = pl.ds(turn * block_rows, block_rows)
-        q = q_ref[rows]
-        q_wide = head_concat(q, heads, group)
-        wide_ref[rows] = q_wide
-        prefix = contract_last(q_wide, keys) * scale + live
-        pieces = []
-        scores = []
-        for i in range(wave * batch):
-            request = turn * wave * batch + i
-            kv = jnp.concatenate(
-                [
-                    suffix_ref[request * cached : (request + 1) * cached],
-                    new_ref[request // batch * fresh : (request // batch + 1) * fresh],
-                ],
-                axis=0,
-            )
-            pieces.append(kv)
-            score = contract_last(q[i * row_heads : (i + 1) * row_heads], kv) * scale
-            scores.append(
-                jnp.where(places[i % batch] < lens_ref[request], score, masked_score)
-            )
-        score = jnp.concatenate(scores, axis=0)
-        row_max = jnp.max(jnp.maximum(prefix, score), axis=1, keepdims=True)
-        weights = jnp.exp2(score - row_max)
-        prefix_weights = jnp.exp2(prefix - row_max)
-        part_ref[rows] = weights + prefix_weights
-        max_ref[rows] = jnp.broadcast_to(row_max, weights.shape)
-        rounded = pltpu.roll(weights, heads, 1).astype(jnp.bfloat16)
-        wide = jnp.dot(
-            prefix_weights.astype(jnp.bfloat16), values, preferred_element_type=jnp.float32
-        )
-        attended = [
-            jnp.dot(
-                rounded[i * row_heads : (i + 1) * row_heads],
-                pieces[i],
-                preferred_element_type=jnp.float32,
-            )
-            for i in range(wave * batch)
-        ]
-        acc_ref[rows] = jnp.concatenate(attended, axis=0) + head_select(wide, heads, group)
+    for request in range(lens_ref.shape[0]):
+        mask_ref[request * row_heads : (request + 1) * row_heads] = jnp.where(
+            places[request % batch] < lens_ref[request], 0.0, masked_score
+        )
+    for copy in copies[2:4]:
+        copy.wait()
+    fill_tables([own_ref], order, keys_ref, values_ref, heads, page)
+    wide_ref[...] = head_concat(q_ref[...], heads, group)
+    for copy in copies[4:]:
+        copy.wait()
+
+
+def local_body(sizes, *refs):
+    heads, group, suffix, scale, batch = sizes
+    q_ref, suffix_ref, new_ref, keys_ref, values_ref, wide_ref, mask_ref, bias_ref = refs[:8]
+    acc_ref, max_ref, part_ref = refs[8:]
+    kinds = 2 * heads
+    row_heads = heads * group
+    cached = suffix * kinds
+    fresh = batch * kinds
+    live = bias_ref[:1, : keys_ref.shape[0]]
+    prefix = contract_last(wide_ref[...], keys_ref[...]) * scale + live
+    pieces = []
+    scores = []
+    for request in range(q_ref.shape[0] // row_heads):
+        kv = jnp.concatenate(
+            [
+                suffix_ref[request * cached : (request + 1) * cached],
+                new_ref[request // batch * fresh : (request // batch + 1) * fresh],
+            ],
+            axis=0,
+        )
+        pieces.append(kv)
+        rows = slice(request * row_heads, (request + 1) * row_heads)
+        scores.append(contract_last(q_ref[rows], kv) * scale + mask_ref[rows])
+    score = jnp.concatenate(scores, axis=0)
+    row_max = jnp.max(jnp.maximum(prefix, score), axis=1, keepdims=True)
+    weights = jnp.exp2(score - row_max)
+    prefix_weights = jnp.exp2(prefix - row_max)
+    part_ref[...] = weights + prefix_weights
+    max_ref[...] = jnp.broadcast_to(row_max, weights.shape)
+    rounded = pltpu.roll(weights, heads, 1).astype(jnp.bfloat16)
+    wide = jnp.dot(
+        prefix_weights.astype(jnp.bfloat16), values_ref[...], preferred_element_type=jnp.float32
+    )
+    attended = [
+        jnp.dot(
+            rounded[i * row_heads : (i + 1) * row_heads],
+            piece,
+            preferred_element_type=jnp.float32,
+        )
+        for i, piece in enumerate(pieces)
+    ]
+    acc_ref[...] = jnp.concatenate(attended, axis=0) + head_select(wide, heads, group)
 
 
 def absorb(sizes, rows, wide_ref, acc_ref, max_ref, part_ref, keys, values, live):
@@ -269,17 +270,6 @@
     return owner
 
 
-def ring_start(raw, replicas):
-    ring = folded_ring(replicas)
-    owners = [ring_owner(ring, step) for step in (1, -1, 2)]
-    return ring_step(raw, ring, 1), ring_step(raw, ring, -1), owners
-
-
-def ring_finish(ahead, back, replicas, anchor):
-    ahead, anchor = lax.optimization_barrier((ahead, anchor))
-    return [[ahead, back], [ring_step(ahead, folded_ring(replicas), 1)]], anchor
-
-
 def gathered_stages(raw, replicas):
     everything = lax.all_gather(raw, "replica", axis=0, tiled=True)
     owners = [lambda me, n, at=at: jnp.where(me == at, -1, at) for at in range(replicas)]
@@ -298,13 +288,14 @@
     scale = width**-0.5 * math.log2(math.e)
     raw = prefix_pool.reshape(slots * page * kinds, width)
     batch = (-suffix * kinds) % lanes // kinds
-    wave = requests // batch
     block_rows = 256
     rows = requests * head_count
     block_tokens = slots * page
     two_ways = replicas == 4
     if two_ways:
-        ahead, back, owners = ring_start(raw, replicas)
+        ring = folded_ring(replicas)
+        ahead = ring_step(raw, ring, 1)
+        owners = [ring_owner(ring, step) for step in (1, -1, 2)]
     else:
         stages, owners = gathered_stages(raw, replicas)
     suffix_rows = requests * suffix * kinds
@@ -319,32 +310,32 @@
     def tables(tokens):
         return [pltpu.VMEM((tokens, heads * width), jnp.bfloat16)] * 2
 
-    acc, row_max, part, q_wide, bias = pl.pallas_call(
-        functools.partial(
-            local_body, (heads, group, page, suffix, scale, batch, replicas, wave), owners
-        ),
+    def low(*shape):
+        return jax.ShapeDtypeStruct(shape, jnp.bfloat16)
+
+    loaded = pl.pallas_call(
+        functools.partial(load_body, (heads, group, page, suffix, batch, replicas), owners),
         out_shape=[
+            low(rows, width),
+            low(suffix_rows, width),
+            low(requests * kinds, width),
+            low(block_tokens, heads * width),
+            low(block_tokens, heads * width),
+            low(rows, heads * width),
             full,
-            full,
-            full,
-            jax.ShapeDtypeStruct((rows, heads * width), jnp.bfloat16),
-            jax.ShapeDtypeStruct((8, len(owners) * block_tokens), jnp.float32),
+            jax.ShapeDtypeStruct((8, (1 + len(owners)) * block_tokens), jnp.float32),
         ],
         in_specs=[hbm()] * 6,
-        out_specs=[vmem()] * 5,
+        out_specs=[vmem()] * 8,
         scratch_shapes=[
             pltpu.SMEM(page_table.shape, jnp.int32),
             pltpu.SMEM(suffix_len.shape, jnp.int32),
-            pltpu.VMEM((rows, width), jnp.bfloat16),
             pltpu.VMEM(raw.shape, jnp.bfloat16),
-            pltpu.VMEM((suffix_rows, width), jnp.bfloat16),
-            pltpu.VMEM((requests * kinds, width), jnp.bfloat16),
-            *tables(block_tokens),
-            pltpu.SemaphoreType.DMA((5 + requests // batch // wave,)),
+            pltpu.SemaphoreType.DMA((6,)),
         ],
         compiler_params=params,
-        cost_estimate=cost(2 * block_tokens),
-        name="local_part",
+        cost_estimate=cost(block_tokens),
+        name="load_part",
     )(
         *[
             pltpu.with_memory_space_constraint(value, pltpu.HBM)
@@ -358,10 +349,24 @@
             )
         ]
     )
+    q_wide, bias = loaded[5], loaded[7]
     if two_ways:
-        stages, acc = ring_finish(ahead, back, replicas, acc)
+        own, bias = lax.optimization_barrier((raw, bias))
+        back = ring_step(own, ring, -1)
+    acc, row_max, part = pl.pallas_call(
+        functools.partial(local_body, (heads, group, suffix, scale, batch)),
+        out_shape=[full] * 3,
+        in_specs=[vmem()] * 8,
+        out_specs=[vmem()] * 3,
+        compiler_params=params,
+        cost_estimate=cost(2 * block_tokens),
+        name="local_part",
+    )(*loaded[:7], bias)
+    if two_ways:
+        ahead, acc = lax.optimization_barrier((ahead, acc))
+        stages = [[ahead, back], [ring_step(ahead, ring, 1)]]
     sizes = (heads, group, page, scale, block_rows, replicas)
-    place = 0
+    place = block_tokens
     count = jnp.broadcast_to(counts, (8, lanes)) if len(stages) == 1 else counts.reshape(1, 1)
     for blocks in stages[:-1]:
         tokens = sum(block.shape[0] for block in blocks) // kinds

time: 16.1 us -> 16.1 us (level)
    pallas_call x1 -> x2, Pallas kernels: 3.68 us -> 3.68 us  [the longest x1 2.03 us: shards(): pl.pallas_call(functools.partial(local_body, (heads, group, suffix, scale...]
where the time goes in v3:
time: 16.1 us; the launch traced here: 16 us
  starting transfers between devices  7.37 us (46%)
  Pallas kernels  6.12 us (38%)
  waiting for transfers between devices  1.78 us (11%)
  between operations  0.69 us (4%)
    ppermute x3, starting transfers between devices, ring_step(): lax.ppermute(values, 'replica', [(ring[i], ring[(i + step) % len(ring)])...  7.37 us
    pallas_call x1, Pallas kernels, shards(): pl.pallas_call(functools.partial(local_body, (heads, group, suffix, scale...  2.03 us
    ppermute x3, waiting for transfers between devices, ring_step(): lax.ppermute(values, 'replica', [(ring[i], ring[(i + step) % len(ring)])...  1.78 us
    pallas_call x1, Pallas kernels, shards(): pl.pallas_call(functools.partial(load_body, (heads, group, page, suffix,...  1.65 us
    pallas_call x1, Pallas kernels, shards(): pl.pallas_call(functools.partial(finish_body, sizes, place), out_shape=ja...  1.53 us
    pallas_call x1, Pallas kernels, shards(): pl.pallas_call(functools.partial(fold_body, sizes, place), out_shape=[jax...  0.91 us
  transfers between devices with their start and end apart: 3, of which 2 were waited for; matrix products, arithmetic and copies ran while one was open for 0% of the time, Pallas kernels for 29%

profile of v3, /device:TPU:0, one launch (start us, length us, event | category | flops | bytes accessed | tf_op | source)
XLA Modules:
  0.0 16.0 jit_solution(11562953804275634316)
XLA Ops:
  0.0 0.0 copy-start
  0.0 4.0 %collective-permute-start = (bf16[512,128]{1,0:T(8,128)(2,1)}, bf16[512,128]{1,0:T(8,128)(2,1)S(1)}, u32[]{:S(2)}, u32[]{:S(2)}) collective-permute-start(bf16[512,128]{1,0:T(8,128)(2,1)} %bitcast.9), channel_id=1, source_target_pairs={{0,8},{8,12},{12,4},{4,0},{1,9},{9,13},{13,5},{5,1},{2,10},{10,14}... | collective-permute-start | bytes 393224 | tf_op jit(solution)/shard_map/ppermute | solution.py:258
  4.0 1.7 %load_part.1 = (bf16[1024,128]{1,0:T(8,128)(2,1)S(1)}, bf16[6144,128]{1,0:T(8,128)(2,1)S(1)}, bf16[256,128]{1,0:T(8,128)(2,1)S(1)}, bf16[128,256]{1,0:T(8,128)(2...) custom-call(s32[6]{0:T(128)} %refs_0_.1, ...), custom_call_target="tpu_custom_call" | custom-call | flops 67108864 | bytes 3145728 | tf_op jit(solution)/shard_map/load_part/pallas_call | solution.py:316
  5.7 0.0 copy-done
  5.7 0.1 collective-permute-start.1
  5.8 2.0 %local_part.1 = (f32[1024,128]{1,0:T(8,128)S(1)}, f32[1024,128]{1,0:T(8,128)S(1)}, f32[1024,128]{1,0:T(8,128)S(1)}) custom-call(bf16[1024,128]{1,0:T(8,128)(2,1)S(1)} %get-tuple-element.25.refs_0_, bf16[6144,128]{1,0:T(8,128)(2,1)S(1)} %get-tuple-element.26.refs_1_, bf16[256,128]{1,0:T(8,128)(2,1)S(1)} %get-tuple-element.27.refs_2_, ...), custom_call_target="tpu_custom_call" | custom-call | flops 134217728 | bytes 3145728 | tf_op jit(solution)/shard_map/local_part/pallas_call | solution.py:356
  7.8 0.5 %collective-permute-done.refs_6_ = bf16[512,128]{1,0:T(8,128)(2,1)S(1)} collective-permute-done((bf16[512,128]{1,0:T(8,128)(2,1)}, bf16[512,128]{1,0:T(8,128)(2,1)S(1)}, u32[]{:S(2)}, u32[]{:S(2)}) %collective-permute-start) | collective-permute-done | bytes 131104 | tf_op jit(solution)/shard_map/ppermute | solution.py:258
  8.3 3.3 %collective-permute-start.2 = (bf16[512,128]{1,0:T(8,128)(2,1)S(1)}, bf16[512,128]{1,0:T(8,128)(2,1)S(1)}, u32[]{:S(2)}, u32[]{:S(2)}) collective-permute-start(bf16[512,128]{1,0:T(8,128)(2,1)S(1)} %collective-permute-done.refs_6_), channel_id=1, source_target_pairs={{0,8},{8,12},{12,4},{4,0},{1,9},{9,13},{13,5},{5,1},{2,10},{10,14}... | collective-permute-start | bytes 393224 | tf_op jit(solution)/shard_map/ppermute | solution.py:258
  12.2 0.0 collective-permute-done.1.refs_7_
  12.2 0.9 %fold_part.1 = (s32[8,128]{1,0:T(8,128)S(1)}, f32[1024,128]{1,0:T(8,128)S(1)}, f32[1024,128]{1,0:T(8,128)S(1)}, f32[1024,128]{1,0:T(8,128)S(1)}) custom-call(s32[1,1]{1,0:T(1,128)} %bitcast.6.refs_0_, bf16[1024,256]{1,0:T(8,128)(2,1)S(1)} %get-tuple-element.24.refs_5_.refs_1_, f32[1024,128]{1,0:T(8,128)S(1)} %get-tuple-element.34.refs_2_, ...), custom_call_target="tpu_custom_call" | custom-call | flops 134217728 | bytes 3145728 | tf_op jit(solution)/shard_map/fold_part/pallas_call | solution.py:373
  13.1 1.3 %collective-permute-done.2.refs_6_ = bf16[512,128]{1,0:T(8,128)(2,1)S(1)} collective-permute-done((bf16[512,128]{1,0:T(8,128)(2,1)S(1)}, bf16[512,128]{1,0:T(8,128)(2,1)S(1)}, u32[]{:S(2)}, u32[]{:S(2)}) %collective-permute-start.2) | collective-permute-done | bytes 131104 | tf_op jit(solution)/shard_map/ppermute | solution.py:258
  14.4 1.5 %finish_part.1 = bf16[1024,128]{1,0:T(8,128)(2,1)} custom-call(s32[8,128]{1,0:T(8,128)S(1)} %get-tuple-element.39.refs_0_, bf16[1024,256]{1,0:T(8,128)(2,1)S(1)} %get-tuple-element.24.refs_5_.refs_1_, f32[1024,128]{1,0:T(8,128)S(1)} %get-tuple-element.40.refs_2_, f32[1024,128]{1,0:T(8,128)S(1)} %get-tuple-element.41.refs_3_, ...), custom_call_target="tpu_custom_call" | custom-call | flops 67108864 | bytes 3145728 | tf_op jit(solution)/shard_map/finish_part/pallas_call | solution.py:385
Async XLA Ops:
  0.0 5.7 %copy-start = (bf16[2,64,2,2,128]{4,3,2,1,0:T(2,128)(2,1)S(1)}, bf16[2,64,2,2,128]{4,3,2,1,0:T(2,128)(2,1)}, u32[]{:S(2)}) copy-start(bf16[2,64,2,2,128]{4,3,2,1,0:T(2,128)(2,1)} %param.8) | copy-start | bytes 393220
  0.0 8.3 %collective-permute-start = (bf16[512,128]{1,0:T(8,128)(2,1)}, bf16[512,128]{1,0:T(8,128)(2,1)S(1)}, u32[]{:S(2)}, u32[]{:S(2)}) collective-permute-start(bf16[512,128]{1,0:T(8,128)(2,1)} %bitcast.9), channel_id=1, source_target_pairs={{0,8},{8,12},{12,4},{4,0},{1,9},{9,13},{13,5},{5,1},{2,10},{10,14}... | collective-permute-start | bytes 393224 | tf_op jit(solution)/shard_map/ppermute | solution.py:258
  5.7 6.5 %collective-permute-start.1 = (bf16[512,128]{1,0:T(8,128)(2,1)S(1)}, bf16[512,128]{1,0:T(8,128)(2,1)S(1)}, u32[]{:S(2)}, u32[]{:S(2)}) collective-permute-start(bf16[512,128]{1,0:T(8,128)(2,1)S(1)} %bitcast.11), channel_id=1, source_target_pairs={{0,4},{8,0},{12,8},{4,12},{1,5},{9,1},{13,9},{5,13},{2,6},{10,2},{... | collective-permute-start | bytes 393224 | tf_op jit(solution)/shard_map/ppermute | solution.py:258
  8.3 6.2 %collective-permute-start.2 = (bf16[512,128]{1,0:T(8,128)(2,1)S(1)}, bf16[512,128]{1,0:T(8,128)(2,1)S(1)}, u32[]{:S(2)}, u32[]{:S(2)}) collective-permute-start(bf16[512,128]{1,0:T(8,128)(2,1)S(1)} %collective-permute-done.refs_6_), channel_id=1, source_target_pairs={{0,8},{8,12},{12,4},{4,0},{1,9},{9,13},{13,5},{5,1},{2,10},{10,14}... | collective-permute-start | bytes 393224 | tf_op jit(solution)/shard_map/ppermute | solution.py:258

commit v4 on v3

--- a/solution.py
+++ b/solution.py
@@ -294,8 +294,8 @@
     two_ways = replicas == 4
     if two_ways:
         ring = folded_ring(replicas)
-        ahead = ring_step(raw, ring, 1)
-        owners = [ring_owner(ring, step) for step in (1, -1, 2)]
+        ahead, back = ring_step(raw, ring, -1), ring_step(raw, ring, 1)
+        owners = [ring_owner(ring, step) for step in (-1, 1, 2)]
     else:
         stages, owners = gathered_stages(raw, replicas)
     suffix_rows = requests * suffix * kinds
@@ -351,8 +351,8 @@
     )
     q_wide, bias = loaded[5], loaded[7]
     if two_ways:
-        own, bias = lax.optimization_barrier((raw, bias))
-        back = ring_step(own, ring, -1)
+        ahead, bias = lax.optimization_barrier((ahead, bias))
+        passed = ring_step(ahead, ring, -1)
     acc, row_max, part = pl.pallas_call(
         functools.partial(local_body, (heads, group, suffix, scale, batch)),
         out_shape=[full] * 3,
@@ -363,8 +363,7 @@
         name="local_part",
     )(*loaded[:7], bias)
     if two_ways:
-        ahead, acc = lax.optimization_barrier((ahead, acc))
-        stages = [[ahead, back], [ring_step(ahead, ring, 1)]]
+        stages = [[ahead, back], [passed]]
     sizes = (heads, group, page, scale, block_rows, replicas)
     place = block_tokens
     count = jnp.broadcast_to(counts, (8, lanes)) if len(stages) == 1 else counts.reshape(1, 1)

time: 16.1 us -> 17.1 us (1.062)
  the two profiles are of different devices: /device:TPU:0 before, /device:TPU:8 now
where the time goes in v4:
time: 17.1 us; the launch traced here: 16.9 us
  Pallas kernels  6.13 us (36%)
  starting transfers between devices  5.87 us (34%)
  waiting for transfers between devices  4.23 us (25%)
  between operations  0.68 us (4%)
    ppermute x3, starting transfers between devices, ring_step(): lax.ppermute(values, 'replica', [(ring[i], ring[(i + step) % len(ring)])...  5.87 us
    ppermute x3, waiting for transfers between devices, ring_step(): lax.ppermute(values, 'replica', [(ring[i], ring[(i + step) % len(ring)])...  4.23 us
    pallas_call x1, Pallas kernels, shards(): pl.pallas_call(functools.partial(local_body, (heads, group, suffix, scale...  2.03 us
    pallas_call x1, Pallas kernels, shards(): pl.pallas_call(functools.partial(load_body, (heads, group, page, suffix,...  1.64 us
    pallas_call x1, Pallas kernels, shards(): pl.pallas_call(functools.partial(finish_body, sizes, place), out_shape=ja...  1.53 us
    pallas_call x1, Pallas kernels, shards(): pl.pallas_call(functools.partial(fold_body, sizes, place), out_shape=[jax...  0.92 us
  transfers between devices with their start and end apart: 3, of which 1 were waited for; matrix products, arithmetic and copies ran while one was open for 0% of the time, Pallas kernels for 27%

profile of v4, /device:TPU:8, one launch (start us, length us, event | category | flops | bytes accessed | tf_op | source)
XLA Modules:
  0.0 16.9 jit_solution(15914024791350953345)
XLA Ops:
  0.0 2.6 %collective-permute-start = (bf16[512,128]{1,0:T(8,128)(2,1)}, bf16[512,128]{1,0:T(8,128)(2,1)S(1)}, u32[]{:S(2)}, u32[]{:S(2)}) collective-permute-start(bf16[512,128]{1,0:T(8,128)(2,1)} %bitcast.9), channel_id=1, source_target_pairs={{0,4},{8,0},{12,8},{4,12},{1,5},{9,1},{13,9},{5,13},{2,6},{10,2},{... | collective-permute-start | bytes 393224 | tf_op jit(solution)/shard_map/ppermute | solution.py:258
  2.6 0.0 collective-permute-start.1
  2.6 1.6 %load_part.1 = (bf16[1024,128]{1,0:T(8,128)(2,1)S(1)}, bf16[6144,128]{1,0:T(8,128)(2,1)S(1)}, bf16[256,128]{1,0:T(8,128)(2,1)S(1)}, bf16[128,256]{1,0:T(8,128)(2...) custom-call(s32[6]{0:T(128)} %refs_0_.1, ...), custom_call_target="tpu_custom_call" | custom-call | flops 67108864 | bytes 3145728 | tf_op jit(solution)/shard_map/load_part/pallas_call | solution.py:316
  4.2 4.2 %collective-permute-done.refs_6_ = bf16[512,128]{1,0:T(8,128)(2,1)S(1)} collective-permute-done((bf16[512,128]{1,0:T(8,128)(2,1)}, bf16[512,128]{1,0:T(8,128)(2,1)S(1)}, u32[]{:S(2)}, u32[]{:S(2)}) %collective-permute-start) | collective-permute-done | bytes 131104 | tf_op jit(solution)/shard_map/ppermute | solution.py:258
  8.5 3.3 %collective-permute-start.2 = (bf16[512,128]{1,0:T(8,128)(2,1)S(1)}, bf16[512,128]{1,0:T(8,128)(2,1)S(1)}, u32[]{:S(2)}, u32[]{:S(2)}) collective-permute-start(bf16[512,128]{1,0:T(8,128)(2,1)S(1)} %collective-permute-done.refs_6_), channel_id=1, source_target_pairs={{0,4},{8,0},{12,8},{4,12},{1,5},{9,1},{13,9},{5,13},{2,6},{10,2},{... | collective-permute-start | bytes 393224 | tf_op jit(solution)/shard_map/ppermute | solution.py:258
  12.4 2.0 %local_part.1 = (f32[1024,128]{1,0:T(8,128)S(1)}, f32[1024,128]{1,0:T(8,128)S(1)}, f32[1024,128]{1,0:T(8,128)S(1)}) custom-call(bf16[1024,128]{1,0:T(8,128)(2,1)S(1)} %get-tuple-element.23.refs_0_, bf16[6144,128]{1,0:T(8,128)(2,1)S(1)} %get-tuple-element.24.refs_1_, bf16[256,128]{1,0:T(8,128)(2,1)S(1)} %get-tuple-element.25.refs_2_, ...), custom_call_target="tpu_custom_call" | custom-call | flops 134217728 | bytes 3145728 | tf_op jit(solution)/shard_map/local_part/pallas_call | solution.py:356
  14.4 0.0 collective-permute-done.1.refs_7_
  14.4 0.9 %fold_part.1 = (s32[8,128]{1,0:T(8,128)S(1)}, f32[1024,128]{1,0:T(8,128)S(1)}, f32[1024,128]{1,0:T(8,128)S(1)}, f32[1024,128]{1,0:T(8,128)S(1)}) custom-call(s32[1,1]{1,0:T(1,128)} %bitcast.6.refs_0_, bf16[1024,256]{1,0:T(8,128)(2,1)S(1)} %get-tuple-element.22.refs_5_.refs_1_, f32[1024,128]{1,0:T(8,128)S(1)} %get-tuple-element.31.refs_2_, ...), custom_call_target="tpu_custom_call" | custom-call | flops 134217728 | bytes 3145728 | tf_op jit(solution)/shard_map/fold_part/pallas_call | solution.py:372
  15.4 0.0 collective-permute-done.2.refs_6_
  15.4 1.5 %finish_part.1 = bf16[1024,128]{1,0:T(8,128)(2,1)} custom-call(s32[8,128]{1,0:T(8,128)S(1)} %get-tuple-element.35.refs_0_, bf16[1024,256]{1,0:T(8,128)(2,1)S(1)} %get-tuple-element.22.refs_5_.refs_1_, f32[1024,128]{1,0:T(8,128)S(1)} %get-tuple-element.36.refs_2_, f32[1024,128]{1,0:T(8,128)S(1)} %get-tuple-element.37.refs_3_, ...), custom_call_target="tpu_custom_call" | custom-call | flops 67108864 | bytes 3145728 | tf_op jit(solution)/shard_map/finish_part/pallas_call | solution.py:384
Async XLA Ops:
  0.0 8.5 %collective-permute-start = (bf16[512,128]{1,0:T(8,128)(2,1)}, bf16[512,128]{1,0:T(8,128)(2,1)S(1)}, u32[]{:S(2)}, u32[]{:S(2)}) collective-permute-start(bf16[512,128]{1,0:T(8,128)(2,1)} %bitcast.9), channel_id=1, source_target_pairs={{0,4},{8,0},{12,8},{4,12},{1,5},{9,1},{13,9},{5,13},{2,6},{10,2},{... | collective-permute-start | bytes 393224 | tf_op jit(solution)/shard_map/ppermute | solution.py:258
  2.6 11.8 %collective-permute-start.1 = (bf16[512,128]{1,0:T(8,128)(2,1)}, bf16[512,128]{1,0:T(8,128)(2,1)S(1)}, u32[]{:S(2)}, u32[]{:S(2)}) collective-permute-start(bf16[512,128]{1,0:T(8,128)(2,1)} %bitcast.10), channel_id=1, source_target_pairs={{0,8},{8,12},{12,4},{4,0},{1,9},{9,13},{13,5},{5,1},{2,10},{10,14}... | collective-permute-start | bytes 393224 | tf_op jit(solution)/shard_map/ppermute | solution.py:258
  8.5 6.9 %collective-permute-start.2 = (bf16[512,128]{1,0:T(8,128)(2,1)S(1)}, bf16[512,128]{1,0:T(8,128)(2,1)S(1)}, u32[]{:S(2)}, u32[]{:S(2)}) collective-permute-start(bf16[512,128]{1,0:T(8,128)(2,1)S(1)} %collective-permute-done.refs_6_), channel_id=1, source_target_pairs={{0,4},{8,0},{12,8},{4,12},{1,5},{9,1},{13,9},{5,13},{2,6},{10,2},{... | collective-permute-start | bytes 393224 | tf_op jit(solution)/shard_map/ppermute | solution.py:258

commit v5 on v3

--- a/solution.py
+++ b/solution.py
@@ -294,8 +294,8 @@
     two_ways = replicas == 4
     if two_ways:
         ring = folded_ring(replicas)
-        ahead = ring_step(raw, ring, 1)
-        owners = [ring_owner(ring, step) for step in (1, -1, 2)]
+        ahead = ring_step(raw, ring, -1)
+        owners = [ring_owner(ring, step) for step in (-1, 1, 2)]
     else:
         stages, owners = gathered_stages(raw, replicas)
     suffix_rows = requests * suffix * kinds
@@ -352,7 +352,7 @@
     q_wide, bias = loaded[5], loaded[7]
     if two_ways:
         own, bias = lax.optimization_barrier((raw, bias))
-        back = ring_step(own, ring, -1)
+        back = ring_step(own, ring, 1)
     acc, row_max, part = pl.pallas_call(
         functools.partial(local_body, (heads, group, suffix, scale, batch)),
         out_shape=[full] * 3,
@@ -364,7 +364,7 @@
     )(*loaded[:7], bias)
     if two_ways:
         ahead, acc = lax.optimization_barrier((ahead, acc))
-        stages = [[ahead, back], [ring_step(ahead, ring, 1)]]
+        stages = [[ahead, back], [ring_step(ahead, ring, -1)]]
     sizes = (heads, group, page, scale, block_rows, replicas)
     place = block_tokens
     count = jnp.broadcast_to(counts, (8, lanes)) if len(stages) == 1 else counts.reshape(1, 1)

time: 16.1 us -> 17.1 us (1.062)
  waiting for transfers between devices: 1.78 us -> 2.37 us
  starting transfers between devices: 7.37 us -> 7.79 us
    ppermute x3, waiting for transfers between devices: 1.78 us -> 2.37 us  [ring_step(): lax.ppermute(values, 'replica', [(ring[i], ring[(i + step) % len(ring)])...]
    ppermute x3, starting transfers between devices: 7.37 us -> 7.79 us  [ring_step(): lax.ppermute(values, 'replica', [(ring[i], ring[(i + step) % len(ring)])...]
  transfers between devices with their start and end apart: 3 -> 3, of which waited for: 2 -> 1; matrix products, arithmetic and copies ran while one was open for 0% -> 0% of each run, Pallas kernels for 29% -> 27%
where the time goes in v5:
time: 17.1 us; the launch traced here: 17 us
  starting transfers between devices  7.79 us (46%)
  Pallas kernels  6.12 us (36%)
  waiting for transfers between devices  2.37 us (14%)
  between operations  0.69 us (4%)
    ppermute x3, starting transfers between devices, ring_step(): lax.ppermute(values, 'replica', [(ring[i], ring[(i + step) % len(ring)])...  7.79 us
    ppermute x3, waiting for transfers between devices, ring_step(): lax.ppermute(values, 'replica', [(ring[i], ring[(i + step) % len(ring)])...  2.37 us
    pallas_call x1, Pallas kernels, shards(): pl.pallas_call(functools.partial(local_body, (heads, group, suffix, scale...  2.03 us
    pallas_call x1, Pallas kernels, shards(): pl.pallas_call(functools.partial(load_body, (heads, group, page, suffix,...  1.65 us
    pallas_call x1, Pallas kernels, shards(): pl.pallas_call(functools.partial(finish_body, sizes, place), out_shape=ja...  1.53 us
    pallas_call x1, Pallas kernels, shards(): pl.pallas_call(functools.partial(fold_body, sizes, place), out_shape=[jax...  0.91 us
  transfers between devices with their start and end apart: 3, of which 1 were waited for; matrix products, arithmetic and copies ran while one was open for 0% of the time, Pallas kernels for 27%

profile of v5, /device:TPU:0, one launch (start us, length us, event | category | flops | bytes accessed | tf_op | source)
XLA Modules:
  0.0 17.0 jit_solution(14478585685410687936)
XLA Ops:
  0.0 0.0 copy-start
  0.0 3.0 %collective-permute-start = (bf16[512,128]{1,0:T(8,128)(2,1)}, bf16[512,128]{1,0:T(8,128)(2,1)S(1)}, u32[]{:S(2)}, u32[]{:S(2)}) collective-permute-start(bf16[512,128]{1,0:T(8,128)(2,1)} %bitcast.9), channel_id=1, source_target_pairs={{0,4},{8,0},{12,8},{4,12},{1,5},{9,1},{13,9},{5,13},{2,6},{10,2},{... | collective-permute-start | bytes 393224 | tf_op jit(solution)/shard_map/ppermute | solution.py:258
  3.0 1.7 %load_part.1 = (bf16[1024,128]{1,0:T(8,128)(2,1)S(1)}, bf16[6144,128]{1,0:T(8,128)(2,1)S(1)}, bf16[256,128]{1,0:T(8,128)(2,1)S(1)}, bf16[128,256]{1,0:T(8,128)(2...) custom-call(s32[6]{0:T(128)} %refs_0_.1, ...), custom_call_target="tpu_custom_call" | custom-call | flops 67108864 | bytes 3145728 | tf_op jit(solution)/shard_map/load_part/pallas_call | solution.py:316
  4.7 0.0 copy-done
  4.7 1.1 %collective-permute-start.1 = (bf16[512,128]{1,0:T(8,128)(2,1)S(1)}, bf16[512,128]{1,0:T(8,128)(2,1)S(1)}, u32[]{:S(2)}, u32[]{:S(2)}) collective-permute-start(bf16[512,128]{1,0:T(8,128)(2,1)S(1)} %bitcast.11), channel_id=1, source_target_pairs={{0,8},{8,12},{12,4},{4,0},{1,9},{9,13},{13,5},{5,1},{2,10},{10,14}... | collective-permute-start | bytes 393224 | tf_op jit(solution)/shard_map/ppermute | solution.py:258
  5.8 2.0 %local_part.1 = (f32[1024,128]{1,0:T(8,128)S(1)}, f32[1024,128]{1,0:T(8,128)S(1)}, f32[1024,128]{1,0:T(8,128)S(1)}) custom-call(bf16[1024,128]{1,0:T(8,128)(2,1)S(1)} %get-tuple-element.25.refs_0_, bf16[6144,128]{1,0:T(8,128)(2,1)S(1)} %get-tuple-element.26.refs_1_, bf16[256,128]{1,0:T(8,128)(2,1)S(1)} %get-tuple-element.27.refs_2_, ...), custom_call_target="tpu_custom_call" | custom-call | flops 134217728 | bytes 3145728 | tf_op jit(solution)/shard_map/local_part/pallas_call | solution.py:356
  7.8 0.0 collective-permute-done.refs_6_
  7.8 3.7 %collective-permute-start.2 = (bf16[512,128]{1,0:T(8,128)(2,1)S(1)}, bf16[512,128]{1,0:T(8,128)(2,1)S(1)}, u32[]{:S(2)}, u32[]{:S(2)}) collective-permute-start(bf16[512,128]{1,0:T(8,128)(2,1)S(1)} %collective-permute-done.refs_6_), channel_id=1, source_target_pairs={{0,4},{8,0},{12,8},{4,12},{1,5},{9,1},{13,9},{5,13},{2,6},{10,2},{... | collective-permute-start | bytes 393224 | tf_op jit(solution)/shard_map/ppermute | solution.py:258
  12.1 0.0 collective-permute-done.1.refs_7_
  12.2 0.9 %fold_part.1 = (s32[8,128]{1,0:T(8,128)S(1)}, f32[1024,128]{1,0:T(8,128)S(1)}, f32[1024,128]{1,0:T(8,128)S(1)}, f32[1024,128]{1,0:T(8,128)S(1)}) custom-call(s32[1,1]{1,0:T(1,128)} %bitcast.6.refs_0_, bf16[1024,256]{1,0:T(8,128)(2,1)S(1)} %get-tuple-element.24.refs_5_.refs_1_, f32[1024,128]{1,0:T(8,128)S(1)} %get-tuple-element.34.refs_2_, ...), custom_call_target="tpu_custom_call" | custom-call | flops 134217728 | bytes 3145728 | tf_op jit(solution)/shard_map/fold_part/pallas_call | solution.py:373
  13.1 2.4 %collective-permute-done.2.refs_6_ = bf16[512,128]{1,0:T(8,128)(2,1)S(1)} collective-permute-done((bf16[512,128]{1,0:T(8,128)(2,1)S(1)}, bf16[512,128]{1,0:T(8,128)(2,1)S(1)}, u32[]{:S(2)}, u32[]{:S(2)}) %collective-permute-start.2) | collective-permute-done | bytes 131104 | tf_op jit(solution)/shard_map/ppermute | solution.py:258
  15.4 1.5 %finish_part.1 = bf16[1024,128]{1,0:T(8,128)(2,1)} custom-call(s32[8,128]{1,0:T(8,128)S(1)} %get-tuple-element.39.refs_0_, bf16[1024,256]{1,0:T(8,128)(2,1)S(1)} %get-tuple-element.24.refs_5_.refs_1_, f32[1024,128]{1,0:T(8,128)S(1)} %get-tuple-element.40.refs_2_, f32[1024,128]{1,0:T(8,128)S(1)} %get-tuple-element.41.refs_3_, ...), custom_call_target="tpu_custom_call" | custom-call | flops 67108864 | bytes 3145728 | tf_op jit(solution)/shard_map/finish_part/pallas_call | solution.py:385
Async XLA Ops:
  0.0 4.7 %copy-start = (bf16[2,64,2,2,128]{4,3,2,1,0:T(2,128)(2,1)S(1)}, bf16[2,64,2,2,128]{4,3,2,1,0:T(2,128)(2,1)}, u32[]{:S(2)}) copy-start(bf16[2,64,2,2,128]{4,3,2,1,0:T(2,128)(2,1)} %param.8) | copy-start | bytes 393220
  0.0 7.8 %collective-permute-start = (bf16[512,128]{1,0:T(8,128)(2,1)}, bf16[512,128]{1,0:T(8,128)(2,1)S(1)}, u32[]{:S(2)}, u32[]{:S(2)}) collective-permute-start(bf16[512,128]{1,0:T(8,128)(2,1)} %bitcast.9), channel_id=1, source_target_pairs={{0,4},{8,0},{12,8},{4,12},{1,5},{9,1},{13,9},{5,13},{2,6},{10,2},{... | collective-permute-start | bytes 393224 | tf_op jit(solution)/shard_map/ppermute | solution.py:258
  4.7 7.5 %collective-permute-start.1 = (bf16[512,128]{1,0:T(8,128)(2,1)S(1)}, bf16[512,128]{1,0:T(8,128)(2,1)S(1)}, u32[]{:S(2)}, u32[]{:S(2)}) collective-permute-start(bf16[512,128]{1,0:T(8,128)(2,1)S(1)} %bitcast.11), channel_id=1, source_target_pairs={{0,8},{8,12},{12,4},{4,0},{1,9},{9,13},{13,5},{5,1},{2,10},{10,14}... | collective-permute-start | bytes 393224 | tf_op jit(solution)/shard_map/ppermute | solution.py:258
  7.8 7.6 %collective-permute-start.2 = (bf16[512,128]{1,0:T(8,128)(2,1)S(1)}, bf16[512,128]{1,0:T(8,128)(2,1)S(1)}, u32[]{:S(2)}, u32[]{:S(2)}) collective-permute-start(bf16[512,128]{1,0:T(8,128)(2,1)S(1)} %collective-permute-done.refs_6_), channel_id=1, source_target_pairs={{0,4},{8,0},{12,8},{4,12},{1,5},{9,1},{13,9},{5,13},{2,6},{10,2},{... | collective-permute-start | bytes 393224 | tf_op jit(solution)/shard_map/ppermute | solution.py:258

commit v6 on v2

--- a/solution.py
+++ b/solution.py
@@ -183,6 +183,26 @@
         acc_ref[rows] = jnp.concatenate(attended, axis=0) + head_select(wide, heads, group)
 
 
+def early_body(sizes, owners, *refs):
+    @pl.when(lax.rem(lax.axis_index("tensor"), 2) == 1)
+    def work():
+        local_body(sizes, owners, *refs)
+
+
+def late_body(sizes, owners, *refs):
+    inputs, done, others = refs[:6], refs[6:11], refs[11:]
+    is_done = lax.rem(lax.axis_index("tensor"), 2) == 1
+
+    @pl.when(is_done)
+    def keep():
+        for source, target in zip(done, others[:5]):
+            target[...] = source[...]
+
+    @pl.when(jnp.logical_not(is_done))
+    def work():
+        local_body(sizes, owners, *inputs, *others)
+
+
 def absorb(sizes, rows, wide_ref, acc_ref, max_ref, part_ref, keys, values, live):
     heads, group, scale = sizes
     score = contract_last(wide_ref[rows], keys) * scale + live
@@ -269,17 +289,6 @@
     return owner
 
 
-def ring_start(raw, replicas):
-    ring = folded_ring(replicas)
-    owners = [ring_owner(ring, step) for step in (1, -1, 2)]
-    return ring_step(raw, ring, 1), ring_step(raw, ring, -1), owners
-
-
-def ring_finish(ahead, back, replicas, anchor):
-    ahead, anchor = lax.optimization_barrier((ahead, anchor))
-    return [[ahead, back], [ring_step(ahead, folded_ring(replicas), 1)]], anchor
-
-
 def gathered_stages(raw, replicas):
     everything = lax.all_gather(raw, "replica", axis=0, tiled=True)
     owners = [lambda me, n, at=at: jnp.where(me == at, -1, at) for at in range(replicas)]
@@ -304,7 +313,9 @@
     block_tokens = slots * page
     two_ways = replicas == 4
     if two_ways:
-        ahead, back, owners = ring_start(raw, replicas)
+        ring = folded_ring(replicas)
+        ahead = ring_step(raw, ring, 1)
+        owners = [ring_owner(ring, step) for step in (1, -1, 2)]
     else:
         stages, owners = gathered_stages(raw, replicas)
     suffix_rows = requests * suffix * kinds
@@ -319,47 +330,56 @@
     def tables(tokens):
         return [pltpu.VMEM((tokens, heads * width), jnp.bfloat16)] * 2
 
-    acc, row_max, part, q_wide, bias = pl.pallas_call(
-        functools.partial(
-            local_body, (heads, group, page, suffix, scale, batch, replicas, wave), owners
-        ),
-        out_shape=[
-            full,
-            full,
-            full,
-            jax.ShapeDtypeStruct((rows, heads * width), jnp.bfloat16),
-            jax.ShapeDtypeStruct((8, len(owners) * block_tokens), jnp.float32),
-        ],
-        in_specs=[hbm()] * 6,
-        out_specs=[vmem()] * 5,
-        scratch_shapes=[
-            pltpu.SMEM(page_table.shape, jnp.int32),
-            pltpu.SMEM(suffix_len.shape, jnp.int32),
-            pltpu.VMEM((rows, width), jnp.bfloat16),
-            pltpu.VMEM(raw.shape, jnp.bfloat16),
-            pltpu.VMEM((suffix_rows, width), jnp.bfloat16),
-            pltpu.VMEM((requests * kinds, width), jnp.bfloat16),
-            *tables(block_tokens),
-            pltpu.SemaphoreType.DMA((5 + requests // batch // wave,)),
-        ],
-        compiler_params=params,
-        cost_estimate=cost(2 * block_tokens),
-        name="local_part",
-    )(
-        *[
-            pltpu.with_memory_space_constraint(value, pltpu.HBM)
-            for value in (
-                page_table,
-                suffix_len,
-                queries.reshape(rows, width),
-                raw,
-                suffix_kv.reshape(suffix_rows, width),
-                new_kv.reshape(requests * kinds, width),
-            )
-        ]
-    )
+    operands = [
+        pltpu.with_memory_space_constraint(value, pltpu.HBM)
+        for value in (
+            page_table,
+            suffix_len,
+            queries.reshape(rows, width),
+            raw,
+            suffix_kv.reshape(suffix_rows, width),
+            new_kv.reshape(requests * kinds, width),
+        )
+    ]
+
+    def local_part(body, done):
+        return pl.pallas_call(
+            functools.partial(
+                body, (heads, group, page, suffix, scale, batch, replicas, wave), owners
+            ),
+            out_shape=[
+                full,
+                full,
+                full,
+                jax.ShapeDtypeStruct((rows, heads * width), jnp.bfloat16),
+                jax.ShapeDtypeStruct((8, len(owners) * block_tokens), jnp.float32),
+            ],
+            in_specs=[hbm()] * 6 + [vmem()] * len(done),
+            out_specs=[vmem()] * 5,
+            scratch_shapes=[
+                pltpu.SMEM(page_table.shape, jnp.int32),
+                pltpu.SMEM(suffix_len.shape, jnp.int32),
+                pltpu.VMEM((rows, width), jnp.bfloat16),
+                pltpu.VMEM(raw.shape, jnp.bfloat16),
+                pltpu.VMEM((suffix_rows, width), jnp.bfloat16),
+                pltpu.VMEM((requests * kinds, width), jnp.bfloat16),
+                *tables(block_tokens),
+                pltpu.SemaphoreType.DMA((5 + requests // batch // wave,)),
+            ],
+            compiler_params=params,
+            cost_estimate=cost(2 * block_tokens),
+            name="local_part",
+        )(*operands, *done)
+
     if two_ways:
-        stages, acc = ring_finish(ahead, back, replicas, acc)
+        done = list(local_part(early_body, []))
+        own, done[4] = lax.optimization_barrier((raw, done[4]))
+        back = ring_step(own, ring, -1)
+        acc, row_max, part, q_wide, bias = local_part(late_body, done)
+        ahead, acc = lax.optimization_barrier((ahead, acc))
+        stages = [[ahead, back], [ring_step(ahead, ring, 1)]]
+    else:
+        acc, row_max, part, q_wide, bias = local_part(local_body, [])
     sizes = (heads, group, page, scale, block_rows, replicas)
     place = 0
     count = jnp.broadcast_to(counts, (8, lanes)) if len(stages) == 1 else counts.reshape(1, 1)

time: 16.1 us -> 16.1 us (level)
  starting transfers between devices: 7.31 us -> 7.04 us
    ppermute x3, starting transfers between devices: 7.31 us -> 7.04 us  [ring_step(): lax.ppermute(values, 'replica', [(ring[i], ring[(i + step) % len(ring)])...]
    pallas_call x1 -> x2, Pallas kernels: 3.68 us -> 3.76 us  [local_part(): pl.pallas_call(functools.partial(body, (heads, group, page, suffix, scale...]
  transfers between devices with their start and end apart: 3 -> 3, of which waited for: 2 -> 1; matrix products, arithmetic and copies ran while one was open for 0% -> 0% of each run, Pallas kernels for 29% -> 30%
where the time goes in v6:
time: 16.1 us; the launch traced here: 16 us
  starting transfers between devices  7.04 us (44%)
  Pallas kernels  6.24 us (39%)
  waiting for transfers between devices  1.99 us (12%)
  between operations  0.71 us (4%)
    ppermute x3, starting transfers between devices, ring_step(): lax.ppermute(values, 'replica', [(ring[i], ring[(i + step) % len(ring)])...  7.04 us
    pallas_call x2, Pallas kernels, local_part(): pl.pallas_call(functools.partial(body, (heads, group, page, suffix, scale...  3.76 us
    ppermute x3, waiting for transfers between devices, ring_step(): lax.ppermute(values, 'replica', [(ring[i], ring[(i + step) % len(ring)])...  1.99 us
    pallas_call x1, Pallas kernels, shards(): pl.pallas_call(functools.partial(finish_body, sizes, place), out_shape=ja...  1.51 us
    pallas_call x1, Pallas kernels, shards(): pl.pallas_call(functools.partial(fold_body, sizes, place), out_shape=[jax...  0.96 us
  transfers between devices with their start and end apart: 3, of which 1 were waited for; matrix products, arithmetic and copies ran while one was open for 0% of the time, Pallas kernels for 30%

profile of v6, /device:TPU:0, one launch (start us, length us, event | category | flops | bytes accessed | tf_op | source)
XLA Modules:
  0.0 16.0 jit_solution(3026229959909768191)
XLA Ops:
  0.0 0.0 copy-start
  0.0 4.0 %collective-permute-start = (bf16[512,128]{1,0:T(8,128)(2,1)}, bf16[512,128]{1,0:T(8,128)(2,1)S(1)}, u32[]{:S(2)}, u32[]{:S(2)}) collective-permute-start(bf16[512,128]{1,0:T(8,128)(2,1)} %bitcast.11), channel_id=1, source_target_pairs={{0,8},{8,12},{12,4},{4,0},{1,9},{9,13},{13,5},{5,1},{2,10},{10,14}... | collective-permute-start | bytes 393224 | tf_op jit(solution)/shard_map/ppermute | solution.py:277
  4.0 0.1 local_part.2
  4.1 0.0 copy-done
  4.1 0.1 collective-permute-start.1
  4.2 3.7 %local_part.3 = (f32[1024,128]{1,0:T(8,128)S(1)}, f32[1024,128]{1,0:T(8,128)S(1)}, f32[1024,128]{1,0:T(8,128)S(1)}, bf16[1024,256]{1,0:T(8,128)(2,1)S(1)}, f32[8,384]{1,0:T(8,128)S(1)}) custom-call(s32[6]{0:T(128)} %refs_0_.3, s32[64]{0:T(128)} %refs_1_.3, bf16[1024,128]{1,0:T(8,128)(2,1)} %bitcast.10, bf16[512,128]{1,0:T(8,128)(2,1)} %bitcast.13, ...), custom_call_target="tpu_custom_call" | custom-call | flops 134217728 | bytes 3145728 | tf_op jit(solution)/shard_map/local_part/pallas_call | solution.py:346
  7.9 0.0 collective-permute-done.refs_6_
  7.9 2.9 %collective-permute-start.2 = (bf16[512,128]{1,0:T(8,128)(2,1)S(1)}, bf16[512,128]{1,0:T(8,128)(2,1)S(1)}, u32[]{:S(2)}, u32[]{:S(2)}) collective-permute-start(bf16[512,128]{1,0:T(8,128)(2,1)S(1)} %collective-permute-done.refs_6_), channel_id=1, source_target_pairs={{0,8},{8,12},{12,4},{4,0},{1,9},{9,13},{13,5},{5,1},{2,10},{10,14}... | collective-permute-start | bytes 393224 | tf_op jit(solution)/shard_map/ppermute | solution.py:277
  11.5 0.0 collective-permute-done.1.refs_7_
  11.5 1.0 %fold_part.1 = (s32[8,128]{1,0:T(8,128)S(1)}, f32[1024,128]{1,0:T(8,128)S(1)}, f32[1024,128]{1,0:T(8,128)S(1)}, f32[1024,128]{1,0:T(8,128)S(1)}) custom-call(s32[1,1]{1,0:T(1,128)} %bitcast.6.refs_0_, bf16[1024,256]{1,0:T(8,128)(2,1)S(1)} %get-tuple-element.29.refs_1_, f32[1024,128]{1,0:T(8,128)S(1)} %get-tuple-element.31.refs_2_, ...), custom_call_target="tpu_custom_call" | custom-call | flops 134217728 | bytes 3145728 | tf_op jit(solution)/shard_map/fold_part/pallas_call | solution.py:388
  12.5 2.0 %collective-permute-done.2.refs_6_ = bf16[512,128]{1,0:T(8,128)(2,1)S(1)} collective-permute-done((bf16[512,128]{1,0:T(8,128)(2,1)S(1)}, bf16[512,128]{1,0:T(8,128)(2,1)S(1)}, u32[]{:S(2)}, u32[]{:S(2)}) %collective-permute-start.2) | collective-permute-done | bytes 131104 | tf_op jit(solution)/shard_map/ppermute | solution.py:277
  14.5 1.5 %finish_part.1 = bf16[1024,128]{1,0:T(8,128)(2,1)} custom-call(s32[8,128]{1,0:T(8,128)S(1)} %get-tuple-element.37.refs_0_, bf16[1024,256]{1,0:T(8,128)(2,1)S(1)} %get-tuple-element.29.refs_1_, f32[1024,128]{1,0:T(8,128)S(1)} %get-tuple-element.38.refs_2_, f32[1024,128]{1,0:T(8,128)S(1)} %get-tuple-element.39.refs_3_, ...), custom_call_target="tpu_custom_call" | custom-call | flops 67108864 | bytes 3145728 | tf_op jit(solution)/shard_map/finish_part/pallas_call | solution.py:400
Async XLA Ops:
  0.0 4.1 %copy-start = (bf16[2,64,2,2,128]{4,3,2,1,0:T(2,128)(2,1)S(1)}, bf16[2,64,2,2,128]{4,3,2,1,0:T(2,128)(2,1)}, u32[]{:S(2)}) copy-start(bf16[2,64,2,2,128]{4,3,2,1,0:T(2,128)(2,1)} %param.8) | copy-start | bytes 393220
  0.0 7.9 %collective-permute-start = (bf16[512,128]{1,0:T(8,128)(2,1)}, bf16[512,128]{1,0:T(8,128)(2,1)S(1)}, u32[]{:S(2)}, u32[]{:S(2)}) collective-permute-start(bf16[512,128]{1,0:T(8,128)(2,1)} %bitcast.11), channel_id=1, source_target_pairs={{0,8},{8,12},{12,4},{4,0},{1,9},{9,13},{13,5},{5,1},{2,10},{10,14}... | collective-permute-start | bytes 393224 | tf_op jit(solution)/shard_map/ppermute | solution.py:277
  4.1 7.4 %collective-permute-start.1 = (bf16[512,128]{1,0:T(8,128)(2,1)S(1)}, bf16[512,128]{1,0:T(8,128)(2,1)S(1)}, u32[]{:S(2)}, u32[]{:S(2)}) collective-permute-start(bf16[512,128]{1,0:T(8,128)(2,1)S(1)} %bitcast.14), channel_id=1, source_target_pairs={{0,4},{8,0},{12,8},{4,12},{1,5},{9,1},{13,9},{5,13},{2,6},{10,2},{... | collective-permute-start | bytes 393224 | tf_op jit(solution)/shard_map/ppermute | solution.py:277
  7.9 6.5 %collective-permute-start.2 = (bf16[512,128]{1,0:T(8,128)(2,1)S(1)}, bf16[512,128]{1,0:T(8,128)(2,1)S(1)}, u32[]{:S(2)}, u32[]{:S(2)}) collective-permute-start(bf16[512,128]{1,0:T(8,128)(2,1)S(1)} %collective-permute-done.refs_6_), channel_id=1, source_target_pairs={{0,8},{8,12},{12,4},{4,0},{1,9},{9,13},{13,5},{5,1},{2,10},{10,14}... | collective-permute-start | bytes 393224 | tf_op jit(solution)/shard_map/ppermute | solution.py:277

commit v7 on v6

--- a/solution.py
+++ b/solution.py
@@ -183,24 +183,25 @@
         acc_ref[rows] = jnp.concatenate(attended, axis=0) + head_select(wide, heads, group)
 
 
-def early_body(sizes, owners, *refs):
-    @pl.when(lax.rem(lax.axis_index("tensor"), 2) == 1)
+def my_turn():
+    odd = lax.rem(lax.axis_index("tensor"), 2) == 1
+    return jnp.where(odd, 0, jnp.where(lax.axis_index("replica") == 0, 1, 2))
+
+
+def turn_body(turn, sizes, owners, *refs):
+    mine = my_turn()
+    inputs, refs = refs[:6], refs[6:]
+    if turn > 0:
+        done, refs = refs[:5], refs[5:]
+
+        @pl.when(mine < turn)
+        def keep():
+            for source, target in zip(done, refs[:5]):
+                target[...] = source[...]
+
+    @pl.when(mine == turn)
     def work():
-        local_body(sizes, owners, *refs)
-
-
-def late_body(sizes, owners, *refs):
-    inputs, done, others = refs[:6], refs[6:11], refs[11:]
-    is_done = lax.rem(lax.axis_index("tensor"), 2) == 1
-
-    @pl.when(is_done)
-    def keep():
-        for source, target in zip(done, others[:5]):
-            target[...] = source[...]
-
-    @pl.when(jnp.logical_not(is_done))
-    def work():
-        local_body(sizes, owners, *inputs, *others)
+        local_body(sizes, owners, *inputs, *refs)
 
 
 def absorb(sizes, rows, wide_ref, acc_ref, max_ref, part_ref, keys, values, live):
@@ -372,12 +373,13 @@
         )(*operands, *done)
 
     if two_ways:
-        done = list(local_part(early_body, []))
+        done = list(local_part(functools.partial(turn_body, 0), []))
         own, done[4] = lax.optimization_barrier((raw, done[4]))
         back = ring_step(own, ring, -1)
-        acc, row_max, part, q_wide, bias = local_part(late_body, done)
-        ahead, acc = lax.optimization_barrier((ahead, acc))
+        done = list(local_part(functools.partial(turn_body, 1), done))
+        ahead, done[4] = lax.optimization_barrier((ahead, done[4]))
         stages = [[ahead, back], [ring_step(ahead, ring, 1)]]
+        acc, row_max, part, q_wide, bias = local_part(functools.partial(turn_body, 2), done)
     else:
         acc, row_max, part, q_wide, bias = local_part(local_body, [])
     sizes = (heads, group, page, scale, block_rows, replicas)

time: 16.1 us -> 16.1 us (level)
  starting transfers between devices: 7.04 us -> 6.67 us
  Pallas kernels: 6.24 us -> 6.45 us
    ppermute x3, starting transfers between devices: 7.04 us -> 6.67 us  [ring_step(): lax.ppermute(values, 'replica', [(ring[i], ring[(i + step) % len(ring)])...]
    pallas_call x2 -> x3, Pallas kernels: 3.76 us -> 3.98 us  [local_part(): pl.pallas_call(functools.partial(body, (heads, group, page, suffix, scale...]
  transfers between devices with their start and end apart: 3 -> 3, of which waited for: 1 -> 1; matrix products, arithmetic and copies ran while one was open for 0% -> 0% of each run, Pallas kernels for 30% -> 31%
where the time goes in v7:
time: 16.1 us; the launch traced here: 16 us
  starting transfers between devices  6.67 us (41%)
  Pallas kernels  6.45 us (40%)
  waiting for transfers between devices  2.13 us (13%)
  between operations  0.72 us (4%)
    ppermute x3, starting transfers between devices, ring_step(): lax.ppermute(values, 'replica', [(ring[i], ring[(i + step) % len(ring)])...  6.67 us
    pallas_call x3, Pallas kernels, local_part(): pl.pallas_call(functools.partial(body, (heads, group, page, suffix, scale...  3.98 us
    ppermute x3, waiting for transfers between devices, ring_step(): lax.ppermute(values, 'replica', [(ring[i], ring[(i + step) % len(ring)])...  2.13 us
    pallas_call x1, Pallas kernels, shards(): pl.pallas_call(functools.partial(finish_body, sizes, place), out_shape=ja...  1.51 us
    pallas_call x1, Pallas kernels, shards(): pl.pallas_call(functools.partial(fold_body, sizes, place), out_shape=[jax...  0.96 us
  transfers between devices with their start and end apart: 3, of which 1 were waited for; matrix products, arithmetic and copies ran while one was open for 0% of the time, Pallas kernels for 31%

profile of v7, /device:TPU:0, one launch (start us, length us, event | category | flops | bytes accessed | tf_op | source)
XLA Modules:
  0.0 16.0 jit_solution(9679061292364021128)
XLA Ops:
  0.0 0.0 copy-start
  0.0 4.0 %collective-permute-start = (bf16[512,128]{1,0:T(8,128)(2,1)}, bf16[512,128]{1,0:T(8,128)(2,1)S(1)}, u32[]{:S(2)}, u32[]{:S(2)}) collective-permute-start(bf16[512,128]{1,0:T(8,128)(2,1)} %bitcast.13), channel_id=1, source_target_pairs={{0,8},{8,12},{12,4},{4,0},{1,9},{9,13},{13,5},{5,1},{2,10},{10,14}... | collective-permute-start | bytes 393224 | tf_op jit(solution)/shard_map/ppermute | solution.py:278
  4.0 0.1 local_part.3
  4.1 0.0 copy-done
  4.1 0.1 collective-permute-start.1
  4.2 3.7 %local_part.4 = (f32[1024,128]{1,0:T(8,128)S(1)}, f32[1024,128]{1,0:T(8,128)S(1)}, f32[1024,128]{1,0:T(8,128)S(1)}, bf16[1024,256]{1,0:T(8,128)(2,1)S(1)}, f32[8,384]{1,0:T(8,128)S(1)}) custom-call(s32[6]{0:T(128)} %refs_0_.5, s32[64]{0:T(128)} %refs_1_.5, bf16[1024,128]{1,0:T(8,128)(2,1)} %bitcast.11, bf16[512,128]{1,0:T(8,128)(2,1)} %bitcast.15, ...), custom_call_target="tpu_custom_call" | custom-call | flops 134217728 | bytes 3145728 | tf_op jit(solution)/shard_map/local_part/pallas_call | solution.py:347
  7.9 0.0 collective-permute-done.refs_6_
  7.9 2.6 %collective-permute-start.2 = (bf16[512,128]{1,0:T(8,128)(2,1)S(1)}, bf16[512,128]{1,0:T(8,128)(2,1)S(1)}, u32[]{:S(2)}, u32[]{:S(2)}) collective-permute-start(bf16[512,128]{1,0:T(8,128)(2,1)S(1)} %collective-permute-done.refs_6_), channel_id=1, source_target_pairs={{0,8},{8,12},{12,4},{4,0},{1,9},{9,13},{13,5},{5,1},{2,10},{10,14}... | collective-permute-start | bytes 393224 | tf_op jit(solution)/shard_map/ppermute | solution.py:278
  11.1 0.2 %local_part.5 = (f32[1024,128]{1,0:T(8,128)S(1)}, f32[1024,128]{1,0:T(8,128)S(1)}, f32[1024,128]{1,0:T(8,128)S(1)}, bf16[1024,256]{1,0:T(8,128)(2,1)S(1)}, f32[8,384]{1,0:T(8,128)S(1)}) custom-call(s32[6]{0:T(128)} %refs_0_.5, s32[64]{0:T(128)} %refs_1_.5, bf16[1024,128]{1,0:T(8,128)(2,1)} %bitcast.12, bf16[512,128]{1,0:T(8,128)(2,1)} %bitcast.16, ...), custom_call_target="tpu_custom_call" | custom-call | flops 134217728 | bytes 3145728 | tf_op jit(solution)/shard_map/local_part/pallas_call | solution.py:347
  11.4 0.0 collective-permute-done.1.refs_7_
  11.4 1.0 %fold_part.1 = (s32[8,128]{1,0:T(8,128)S(1)}, f32[1024,128]{1,0:T(8,128)S(1)}, f32[1024,128]{1,0:T(8,128)S(1)}, f32[1024,128]{1,0:T(8,128)S(1)}) custom-call(s32[1,1]{1,0:T(1,128)} %bitcast.6.refs_0_, bf16[1024,256]{1,0:T(8,128)(2,1)S(1)} %get-tuple-element.40.refs_1_, f32[1024,128]{1,0:T(8,128)S(1)} %get-tuple-element.41.refs_2_, ...), custom_call_target="tpu_custom_call" | custom-call | flops 134217728 | bytes 3145728 | tf_op jit(solution)/shard_map/fold_part/pallas_call | solution.py:390
  12.3 2.1 %collective-permute-done.2.refs_6_ = bf16[512,128]{1,0:T(8,128)(2,1)S(1)} collective-permute-done((bf16[512,128]{1,0:T(8,128)(2,1)S(1)}, bf16[512,128]{1,0:T(8,128)(2,1)S(1)}, u32[]{:S(2)}, u32[]{:S(2)}) %collective-permute-start.2) | collective-permute-done | bytes 131104 | tf_op jit(solution)/shard_map/ppermute | solution.py:278
  14.5 1.5 %finish_part.1 = bf16[1024,128]{1,0:T(8,128)(2,1)} custom-call(s32[8,128]{1,0:T(8,128)S(1)} %get-tuple-element.47.refs_0_, bf16[1024,256]{1,0:T(8,128)(2,1)S(1)} %get-tuple-element.40.refs_1_, f32[1024,128]{1,0:T(8,128)S(1)} %get-tuple-element.48.refs_2_, f32[1024,128]{1,0:T(8,128)S(1)} %get-tuple-element.49.refs_3_, ...), custom_call_target="tpu_custom_call" | custom-call | flops 67108864 | bytes 3145728 | tf_op jit(solution)/shard_map/finish_part/pallas_call | solution.py:402
Async XLA Ops:
  0.0 4.1 %copy-start = (bf16[2,64,2,2,128]{4,3,2,1,0:T(2,128)(2,1)S(1)}, bf16[2,64,2,2,128]{4,3,2,1,0:T(2,128)(2,1)}, u32[]{:S(2)}) copy-start(bf16[2,64,2,2,128]{4,3,2,1,0:T(2,128)(2,1)} %param.8) | copy-start | bytes 393220
  0.0 7.9 %collective-permute-start = (bf16[512,128]{1,0:T(8,128)(2,1)}, bf16[512,128]{1,0:T(8,128)(2,1)S(1)}, u32[]{:S(2)}, u32[]{:S(2)}) collective-permute-start(bf16[512,128]{1,0:T(8,128)(2,1)} %bitcast.13), channel_id=1, source_target_pairs={{0,8},{8,12},{12,4},{4,0},{1,9},{9,13},{13,5},{5,1},{2,10},{10,14}... | collective-permute-start | bytes 393224 | tf_op jit(solution)/shard_map/ppermute | solution.py:278
  4.1 7.2 %collective-permute-start.1 = (bf16[512,128]{1,0:T(8,128)(2,1)S(1)}, bf16[512,128]{1,0:T(8,128)(2,1)S(1)}, u32[]{:S(2)}, u32[]{:S(2)}) collective-permute-start(bf16[512,128]{1,0:T(8,128)(2,1)S(1)} %bitcast.17), channel_id=1, source_target_pairs={{0,4},{8,0},{12,8},{4,12},{1,5},{9,1},{13,9},{5,13},{2,6},{10,2},{... | collective-permute-start | bytes 393224 | tf_op jit(solution)/shard_map/ppermute | solution.py:278
  7.9 6.5 %collective-permute-start.2 = (bf16[512,128]{1,0:T(8,128)(2,1)S(1)}, bf16[512,128]{1,0:T(8,128)(2,1)S(1)}, u32[]{:S(2)}, u32[]{:S(2)}) collective-permute-start(bf16[512,128]{1,0:T(8,128)(2,1)S(1)} %collective-permute-done.refs_6_), channel_id=1, source_target_pairs={{0,8},{8,12},{12,4},{4,0},{1,9},{9,13},{13,5},{5,1},{2,10},{10,14}... | collective-permute-start | bytes 393224 | tf_op jit(solution)/shard_map/ppermute | solution.py:278

commit v8 on v2

--- a/solution.py
+++ b/solution.py
@@ -220,13 +220,15 @@
     heads, group, page, scale, block_rows, replicas = sizes
     count_ref, wide_ref, acc_in, max_in, part_in, bias_ref = refs[:6]
     raws = refs[6:-5]
-    out_hbm, out_ref, keys_ref, values_ref, sem = refs[-5:]
+    out_hbm, out_ref, keys_ref, values_ref, sems = refs[-5:]
     kinds = 2 * heads
     fill_tables(raws, page_order(page * kinds, kinds), keys_ref, values_ref, heads, page)
     keys = keys_ref[...]
     values = values_ref[...]
     live = bias_ref[:1, place : place + keys.shape[0]]
     live_rows = count_ref[:1, :] * (heads * group)
+    half = wide_ref.shape[0] // 2
+    copies = []
     for start in range(0, wide_ref.shape[0], block_rows):
         rows = pl.ds(start, block_rows)
         acc, row_max, part = absorb(
@@ -236,9 +238,15 @@
         row = start + lax.broadcasted_iota(jnp.int32, part.shape, 0)
         share = jnp.where(row < live_rows, 1.0 / total, 0.0)
         out_ref[rows] = (acc * share).astype(jnp.bfloat16)
-    copy = pltpu.make_async_copy(out_ref, out_hbm, sem)
-    copy.start()
-    copy.wait()
+        if (start + block_rows) % half == 0:
+            ready = pl.ds(start + block_rows - half, half)
+            place = len(copies)
+            copies.append(
+                pltpu.make_async_copy(out_ref.at[ready], out_hbm.at[ready], sems.at[place])
+            )
+            copies[-1].start()
+    for copy in copies:
+        copy.wait()
 
 
 def vmem():
@@ -385,7 +393,7 @@
         scratch_shapes=[
             pltpu.VMEM((rows, width), jnp.bfloat16),
             *tables(tokens),
-            pltpu.SemaphoreType.DMA,
+            pltpu.SemaphoreType.DMA((2,)),
         ],
         compiler_params=params,
         cost_estimate=cost(tokens),

time: 16.1 us -> 16 us (level)
  no operation moved by 1% of the time
where the time goes in v8:
time: 16 us; the launch traced here: 15.9 us
  starting transfers between devices  7.31 us (46%)
  Pallas kernels  6.06 us (38%)
  waiting for transfers between devices  1.84 us (12%)
  between operations  0.68 us (4%)
    ppermute x3, starting transfers between devices, ring_step(): lax.ppermute(values, 'replica', [(ring[i], ring[(i + step) % len(ring)])...  7.31 us
    pallas_call x1, Pallas kernels, shards(): pl.pallas_call(functools.partial(local_body, (heads, group, page, suffix,...  3.68 us
    ppermute x3, waiting for transfers between devices, ring_step(): lax.ppermute(values, 'replica', [(ring[i], ring[(i + step) % len(ring)])...  1.84 us
    pallas_call x1, Pallas kernels, shards(): pl.pallas_call(functools.partial(finish_body, sizes, place), out_shape=ja...  1.47 us
    pallas_call x1, Pallas kernels, shards(): pl.pallas_call(functools.partial(fold_body, sizes, place), out_shape=[jax...  0.91 us
  transfers between devices with their start and end apart: 3, of which 2 were waited for; matrix products, arithmetic and copies ran while one was open for 0% of the time, Pallas kernels for 29%

profile of v8, /device:TPU:0, one launch (start us, length us, event | category | flops | bytes accessed | tf_op | source)
XLA Modules:
  0.0 15.9 jit_solution(9755135997944039986)
XLA Ops:
  0.0 4.0 %collective-permute-start = (bf16[512,128]{1,0:T(8,128)(2,1)}, bf16[512,128]{1,0:T(8,128)(2,1)S(1)}, u32[]{:S(2)}, u32[]{:S(2)}) collective-permute-start(bf16[512,128]{1,0:T(8,128)(2,1)} %bitcast.9), channel_id=1, source_target_pairs={{0,8},{8,12},{12,4},{4,0},{1,9},{9,13},{13,5},{5,1},{2,10},{10,14}... | collective-permute-start | bytes 393224 | tf_op jit(solution)/shard_map/ppermute | solution.py:265
  4.0 0.0 collective-permute-start.1
  4.0 3.7 %local_part.1 = (f32[1024,128]{1,0:T(8,128)S(1)}, f32[1024,128]{1,0:T(8,128)S(1)}, f32[1024,128]{1,0:T(8,128)S(1)}, bf16[1024,256]{1,0:T(8,128)(2,1)S(1)}, f32[8,384]{1,0:T(8,128)S(1)}) custom-call(s32[6]{0:T(128)} %refs_0_.1, s32[64]{0:T(128)} %refs_1_.1, bf16[1024,128]{1,0:T(8,128)(2,1)} %bitcast.8, bf16[512,128]{1,0:T(8,128)(2,1)} %bitcast.11, ...), custom_call_target="tpu_custom_call" | custom-call | flops 134217728 | bytes 3145728 | tf_op jit(solution)/shard_map/local_part/pallas_call | solution.py:330
  7.7 0.5 %collective-permute-done.refs_6_ = bf16[512,128]{1,0:T(8,128)(2,1)S(1)} collective-permute-done((bf16[512,128]{1,0:T(8,128)(2,1)}, bf16[512,128]{1,0:T(8,128)(2,1)S(1)}, u32[]{:S(2)}, u32[]{:S(2)}) %collective-permute-start) | collective-permute-done | bytes 131104 | tf_op jit(solution)/shard_map/ppermute | solution.py:265
  8.3 3.3 %collective-permute-start.2 = (bf16[512,128]{1,0:T(8,128)(2,1)S(1)}, bf16[512,128]{1,0:T(8,128)(2,1)S(1)}, u32[]{:S(2)}, u32[]{:S(2)}) collective-permute-start(bf16[512,128]{1,0:T(8,128)(2,1)S(1)} %collective-permute-done.refs_6_), channel_id=1, source_target_pairs={{0,8},{8,12},{12,4},{4,0},{1,9},{9,13},{13,5},{5,1},{2,10},{10,14}... | collective-permute-start | bytes 393224 | tf_op jit(solution)/shard_map/ppermute | solution.py:265
  12.2 0.0 collective-permute-done.1.refs_7_
  12.2 0.9 %fold_part.1 = (s32[8,128]{1,0:T(8,128)S(1)}, f32[1024,128]{1,0:T(8,128)S(1)}, f32[1024,128]{1,0:T(8,128)S(1)}, f32[1024,128]{1,0:T(8,128)S(1)}) custom-call(s32[1,1]{1,0:T(1,128)} %bitcast.6.refs_0_, bf16[1024,256]{1,0:T(8,128)(2,1)S(1)} %get-tuple-element.16.refs_1_, f32[1024,128]{1,0:T(8,128)S(1)} %get-tuple-element.18.refs_2_, ...), custom_call_target="tpu_custom_call" | custom-call | flops 134217728 | bytes 3145728 | tf_op jit(solution)/shard_map/fold_part/pallas_call | solution.py:376
  13.1 1.3 %collective-permute-done.2.refs_6_ = bf16[512,128]{1,0:T(8,128)(2,1)S(1)} collective-permute-done((bf16[512,128]{1,0:T(8,128)(2,1)S(1)}, bf16[512,128]{1,0:T(8,128)(2,1)S(1)}, u32[]{:S(2)}, u32[]{:S(2)}) %collective-permute-start.2) | collective-permute-done | bytes 131104 | tf_op jit(solution)/shard_map/ppermute | solution.py:265
  14.4 1.5 %finish_part.1 = bf16[1024,128]{1,0:T(8,128)(2,1)} custom-call(s32[8,128]{1,0:T(8,128)S(1)} %get-tuple-element.23.refs_0_, bf16[1024,256]{1,0:T(8,128)(2,1)S(1)} %get-tuple-element.16.refs_1_, f32[1024,128]{1,0:T(8,128)S(1)} %get-tuple-element.24.refs_2_, f32[1024,128]{1,0:T(8,128)S(1)} %get-tuple-element.25.refs_3_, ...), custom_call_target="tpu_custom_call" | custom-call | flops 67108864 | bytes 3145728 | tf_op jit(solution)/shard_map/finish_part/pallas_call | solution.py:388
Async XLA Ops:
  0.0 8.3 %collective-permute-start = (bf16[512,128]{1,0:T(8,128)(2,1)}, bf16[512,128]{1,0:T(8,128)(2,1)S(1)}, u32[]{:S(2)}, u32[]{:S(2)}) collective-permute-start(bf16[512,128]{1,0:T(8,128)(2,1)} %bitcast.9), channel_id=1, source_target_pairs={{0,8},{8,12},{12,4},{4,0},{1,9},{9,13},{13,5},{5,1},{2,10},{10,14}... | collective-permute-start | bytes 393224 | tf_op jit(solution)/shard_map/ppermute | solution.py:265
  4.0 8.1 %collective-permute-start.1 = (bf16[512,128]{1,0:T(8,128)(2,1)}, bf16[512,128]{1,0:T(8,128)(2,1)S(1)}, u32[]{:S(2)}, u32[]{:S(2)}) collective-permute-start(bf16[512,128]{1,0:T(8,128)(2,1)} %bitcast.10), channel_id=1, source_target_pairs={{0,4},{8,0},{12,8},{4,12},{1,5},{9,1},{13,9},{5,13},{2,6},{10,2},{... | collective-permute-start | bytes 393224 | tf_op jit(solution)/shard_map/ppermute | solution.py:265
  8.3 6.2 %collective-permute-start.2 = (bf16[512,128]{1,0:T(8,128)(2,1)S(1)}, bf16[512,128]{1,0:T(8,128)(2,1)S(1)}, u32[]{:S(2)}, u32[]{:S(2)}) collective-permute-start(bf16[512,128]{1,0:T(8,128)(2,1)S(1)} %collective-permute-done.refs_6_), channel_id=1, source_target_pairs={{0,8},{8,12},{12,4},{4,0},{1,9},{9,13},{13,5},{5,1},{2,10},{10,14}... | collective-permute-start | bytes 393224 | tf_op jit(solution)/shard_map/ppermute | solution.py:265

commit v9 on v7

--- a/solution.py
+++ b/solution.py
@@ -185,7 +185,11 @@
 
 def my_turn():
     odd = lax.rem(lax.axis_index("tensor"), 2) == 1
-    return jnp.where(odd, 0, jnp.where(lax.axis_index("replica") == 0, 1, 2))
+    replica = lax.axis_index("replica")
+    first = lax.rem(replica, 2) == 1
+    return jnp.where(
+        odd, jnp.where(first, 0, 1), jnp.where(replica == 0, 1, 2)
+    )
 
 
 def turn_body(turn, sizes, owners, *refs):

time: 16.1 us -> 15.5 us (0.963)
  the two profiles are of different devices: /device:TPU:0 before, /device:TPU:1 now
where the time goes in v9:
time: 15.5 us; the launch traced here: 15.3 us
  Pallas kernels  6.42 us (41%)
  starting transfers between devices  5.91 us (38%)
  waiting for transfers between devices  2.29 us (15%)
  between operations  0.71 us (5%)
    ppermute x3, starting transfers between devices, ring_step(): lax.ppermute(values, 'replica', [(ring[i], ring[(i + step) % len(ring)])...  5.91 us
    pallas_call x3, Pallas kernels, local_part(): pl.pallas_call(functools.partial(body, (heads, group, page, suffix, scale...  3.96 us
    ppermute x3, waiting for transfers between devices, ring_step(): lax.ppermute(values, 'replica', [(ring[i], ring[(i + step) % len(ring)])...  2.29 us
    pallas_call x1, Pallas kernels, shards(): pl.pallas_call(functools.partial(finish_body, sizes, place), out_shape=ja...  1.51 us
    pallas_call x1, Pallas kernels, shards(): pl.pallas_call(functools.partial(fold_body, sizes, place), out_shape=[jax...  0.95 us
  transfers between devices with their start and end apart: 3, of which 2 were waited for; matrix products, arithmetic and copies ran while one was open for 0% of the time, Pallas kernels for 32%

profile of v9, /device:TPU:1, one launch (start us, length us, event | category | flops | bytes accessed | tf_op | source)
XLA Modules:
  0.0 15.3 jit_solution(15099382480298235065)
XLA Ops:
  0.0 0.0 copy-start
  0.0 3.1 %collective-permute-start = (bf16[512,128]{1,0:T(8,128)(2,1)}, bf16[512,128]{1,0:T(8,128)(2,1)S(1)}, u32[]{:S(2)}, u32[]{:S(2)}) collective-permute-start(bf16[512,128]{1,0:T(8,128)(2,1)} %bitcast.13), channel_id=1, source_target_pairs={{0,8},{8,12},{12,4},{4,0},{1,9},{9,13},{13,5},{5,1},{2,10},{10,14}... | collective-permute-start | bytes 393224 | tf_op jit(solution)/shard_map/ppermute | solution.py:282
  3.1 0.1 local_part.3
  3.2 0.0 copy-done
  3.2 2.7 %collective-permute-start.1 = (bf16[512,128]{1,0:T(8,128)(2,1)S(1)}, bf16[512,128]{1,0:T(8,128)(2,1)S(1)}, u32[]{:S(2)}, u32[]{:S(2)}) collective-permute-start(bf16[512,128]{1,0:T(8,128)(2,1)S(1)} %bitcast.17), channel_id=1, source_target_pairs={{0,4},{8,0},{12,8},{4,12},{1,5},{9,1},{13,9},{5,13},{2,6},{10,2},{... | collective-permute-start | bytes 393224 | tf_op jit(solution)/shard_map/ppermute | solution.py:282
  5.9 3.7 %local_part.4 = (f32[1024,128]{1,0:T(8,128)S(1)}, f32[1024,128]{1,0:T(8,128)S(1)}, f32[1024,128]{1,0:T(8,128)S(1)}, bf16[1024,256]{1,0:T(8,128)(2,1)S(1)}, f32[8,384]{1,0:T(8,128)S(1)}) custom-call(s32[6]{0:T(128)} %refs_0_.5, s32[64]{0:T(128)} %refs_1_.5, bf16[1024,128]{1,0:T(8,128)(2,1)} %bitcast.11, bf16[512,128]{1,0:T(8,128)(2,1)} %bitcast.15, ...), custom_call_target="tpu_custom_call" | custom-call | flops 134217728 | bytes 3145728 | tf_op jit(solution)/shard_map/local_part/pallas_call | solution.py:351
  9.6 0.0 collective-permute-done.refs_6_
  9.6 0.1 collective-permute-start.2
  10.3 0.2 %local_part.5 = (f32[1024,128]{1,0:T(8,128)S(1)}, f32[1024,128]{1,0:T(8,128)S(1)}, f32[1024,128]{1,0:T(8,128)S(1)}, bf16[1024,256]{1,0:T(8,128)(2,1)S(1)}, f32[8,384]{1,0:T(8,128)S(1)}) custom-call(s32[6]{0:T(128)} %refs_0_.5, s32[64]{0:T(128)} %refs_1_.5, bf16[1024,128]{1,0:T(8,128)(2,1)} %bitcast.12, bf16[512,128]{1,0:T(8,128)(2,1)} %bitcast.16, ...), custom_call_target="tpu_custom_call" | custom-call | flops 134217728 | bytes 3145728 | tf_op jit(solution)/shard_map/local_part/pallas_call | solution.py:351
  10.6 0.6 %collective-permute-done.1.refs_7_ = bf16[512,128]{1,0:T(8,128)(2,1)S(1)} collective-permute-done((bf16[512,128]{1,0:T(8,128)(2,1)S(1)}, bf16[512,128]{1,0:T(8,128)(2,1)S(1)}, u32[]{:S(2)}, u32[]{:S(2)}) %collective-permute-start.1) | collective-permute-done | bytes 131104 | tf_op jit(solution)/shard_map/ppermute | solution.py:282
  11.2 1.0 %fold_part.1 = (s32[8,128]{1,0:T(8,128)S(1)}, f32[1024,128]{1,0:T(8,128)S(1)}, f32[1024,128]{1,0:T(8,128)S(1)}, f32[1024,128]{1,0:T(8,128)S(1)}) custom-call(s32[1,1]{1,0:T(1,128)} %bitcast.6.refs_0_, bf16[1024,256]{1,0:T(8,128)(2,1)S(1)} %get-tuple-element.40.refs_1_, f32[1024,128]{1,0:T(8,128)S(1)} %get-tuple-element.41.refs_2_, ...), custom_call_target="tpu_custom_call" | custom-call | flops 134217728 | bytes 3145728 | tf_op jit(solution)/shard_map/fold_part/pallas_call | solution.py:394
  12.2 1.7 %collective-permute-done.2.refs_6_ = bf16[512,128]{1,0:T(8,128)(2,1)S(1)} collective-permute-done((bf16[512,128]{1,0:T(8,128)(2,1)S(1)}, bf16[512,128]{1,0:T(8,128)(2,1)S(1)}, u32[]{:S(2)}, u32[]{:S(2)}) %collective-permute-start.2) | collective-permute-done | bytes 131104 | tf_op jit(solution)/shard_map/ppermute | solution.py:282
  13.8 1.5 %finish_part.1 = bf16[1024,128]{1,0:T(8,128)(2,1)} custom-call(s32[8,128]{1,0:T(8,128)S(1)} %get-tuple-element.47.refs_0_, bf16[1024,256]{1,0:T(8,128)(2,1)S(1)} %get-tuple-element.40.refs_1_, f32[1024,128]{1,0:T(8,128)S(1)} %get-tuple-element.48.refs_2_, f32[1024,128]{1,0:T(8,128)S(1)} %get-tuple-element.49.refs_3_, ...), custom_call_target="tpu_custom_call" | custom-call | flops 67108864 | bytes 3145728 | tf_op jit(solution)/shard_map/finish_part/pallas_call | solution.py:406
Async XLA Ops:
  0.0 3.2 %copy-start = (bf16[2,64,2,2,128]{4,3,2,1,0:T(2,128)(2,1)S(1)}, bf16[2,64,2,2,128]{4,3,2,1,0:T(2,128)(2,1)}, u32[]{:S(2)}) copy-start(bf16[2,64,2,2,128]{4,3,2,1,0:T(2,128)(2,1)} %param.8) | copy-start | bytes 393220
  0.0 9.6 %collective-permute-start = (bf16[512,128]{1,0:T(8,128)(2,1)}, bf16[512,128]{1,0:T(8,128)(2,1)S(1)}, u32[]{:S(2)}, u32[]{:S(2)}) collective-permute-start(bf16[512,128]{1,0:T(8,128)(2,1)} %bitcast.13), channel_id=1, source_target_pairs={{0,8},{8,12},{12,4},{4,0},{1,9},{9,13},{13,5},{5,1},{2,10},{10,14}... | collective-permute-start | bytes 393224 | tf_op jit(solution)/shard_map/ppermute | solution.py:282
  3.2 8.0 %collective-permute-start.1 = (bf16[512,128]{1,0:T(8,128)(2,1)S(1)}, bf16[512,128]{1,0:T(8,128)(2,1)S(1)}, u32[]{:S(2)}, u32[]{:S(2)}) collective-permute-start(bf16[512,128]{1,0:T(8,128)(2,1)S(1)} %bitcast.17), channel_id=1, source_target_pairs={{0,4},{8,0},{12,8},{4,12},{1,5},{9,1},{13,9},{5,13},{2,6},{10,2},{... | collective-permute-start | bytes 393224 | tf_op jit(solution)/shard_map/ppermute | solution.py:282
  9.6 4.2 %collective-permute-start.2 = (bf16[512,128]{1,0:T(8,128)(2,1)S(1)}, bf16[512,128]{1,0:T(8,128)(2,1)S(1)}, u32[]{:S(2)}, u32[]{:S(2)}) collective-permute-start(bf16[512,128]{1,0:T(8,128)(2,1)S(1)} %collective-permute-done.refs_6_), channel_id=1, source_target_pairs={{0,8},{8,12},{12,4},{4,0},{1,9},{9,13},{13,5},{5,1},{2,10},{10,14}... | collective-permute-start | bytes 393224 | tf_op jit(solution)/shard_map/ppermute | solution.py:282

commit v10 on v9

--- a/solution.py
+++ b/solution.py
@@ -188,7 +188,7 @@
     replica = lax.axis_index("replica")
     first = lax.rem(replica, 2) == 1
     return jnp.where(
-        odd, jnp.where(first, 0, 1), jnp.where(replica == 0, 1, 2)
+        odd, jnp.where(first, 0, 2), jnp.where(replica == 0, 1, 2)
     )
 
 

time: 15.5 us -> 16.1 us (1.039)
  the two profiles are of different devices: /device:TPU:1 before, /device:TPU:0 now
where the time goes in v10:
time: 16.1 us; the launch traced here: 16 us
  starting transfers between devices  6.74 us (42%)
  Pallas kernels  6.45 us (40%)
  waiting for transfers between devices  2.05 us (13%)
  between operations  0.71 us (4%)
    ppermute x3, starting transfers between devices, ring_step(): lax.ppermute(values, 'replica', [(ring[i], ring[(i + step) % len(ring)])...  6.74 us
    pallas_call x3, Pallas kernels, local_part(): pl.pallas_call(functools.partial(body, (heads, group, page, suffix, scale...  3.99 us
    ppermute x3, waiting for transfers between devices, ring_step(): lax.ppermute(values, 'replica', [(ring[i], ring[(i + step) % len(ring)])...  2.05 us
    pallas_call x1, Pallas kernels, shards(): pl.pallas_call(functools.partial(finish_body, sizes, place), out_shape=ja...  1.51 us
    pallas_call x1, Pallas kernels, shards(): pl.pallas_call(functools.partial(fold_body, sizes, place), out_shape=[jax...  0.95 us
  transfers between devices with their start and end apart: 3, of which 2 were waited for; matrix products, arithmetic and copies ran while one was open for 0% of the time, Pallas kernels for 31%

profile of v10, /device:TPU:0, one launch (start us, length us, event | category | flops | bytes accessed | tf_op | source)
XLA Modules:
  0.0 16.0 jit_solution(15206711445324801628)
XLA Ops:
  0.0 0.0 copy-start
  0.0 4.0 %collective-permute-start = (bf16[512,128]{1,0:T(8,128)(2,1)}, bf16[512,128]{1,0:T(8,128)(2,1)S(1)}, u32[]{:S(2)}, u32[]{:S(2)}) collective-permute-start(bf16[512,128]{1,0:T(8,128)(2,1)} %bitcast.13), channel_id=1, source_target_pairs={{0,8},{8,12},{12,4},{4,0},{1,9},{9,13},{13,5},{5,1},{2,10},{10,14}... | collective-permute-start | bytes 393224 | tf_op jit(solution)/shard_map/ppermute | solution.py:282
  4.0 0.1 local_part.3
  4.1 0.0 copy-done
  4.1 0.1 collective-permute-start.1
  4.2 3.7 %local_part.4 = (f32[1024,128]{1,0:T(8,128)S(1)}, f32[1024,128]{1,0:T(8,128)S(1)}, f32[1024,128]{1,0:T(8,128)S(1)}, bf16[1024,256]{1,0:T(8,128)(2,1)S(1)}, f32[8,384]{1,0:T(8,128)S(1)}) custom-call(s32[6]{0:T(128)} %refs_0_.5, s32[64]{0:T(128)} %refs_1_.5, bf16[1024,128]{1,0:T(8,128)(2,1)} %bitcast.11, bf16[512,128]{1,0:T(8,128)(2,1)} %bitcast.15, ...), custom_call_target="tpu_custom_call" | custom-call | flops 134217728 | bytes 3145728 | tf_op jit(solution)/shard_map/local_part/pallas_call | solution.py:351
  7.9 0.0 collective-permute-done.refs_6_
  7.9 2.6 %collective-permute-start.2 = (bf16[512,128]{1,0:T(8,128)(2,1)S(1)}, bf16[512,128]{1,0:T(8,128)(2,1)S(1)}, u32[]{:S(2)}, u32[]{:S(2)}) collective-permute-start(bf16[512,128]{1,0:T(8,128)(2,1)S(1)} %collective-permute-done.refs_6_), channel_id=1, source_target_pairs={{0,8},{8,12},{12,4},{4,0},{1,9},{9,13},{13,5},{5,1},{2,10},{10,14}... | collective-permute-start | bytes 393224 | tf_op jit(solution)/shard_map/ppermute | solution.py:282
  11.2 0.2 %local_part.5 = (f32[1024,128]{1,0:T(8,128)S(1)}, f32[1024,128]{1,0:T(8,128)S(1)}, f32[1024,128]{1,0:T(8,128)S(1)}, bf16[1024,256]{1,0:T(8,128)(2,1)S(1)}, f32[8,384]{1,0:T(8,128)S(1)}) custom-call(s32[6]{0:T(128)} %refs_0_.5, s32[64]{0:T(128)} %refs_1_.5, bf16[1024,128]{1,0:T(8,128)(2,1)} %bitcast.12, bf16[512,128]{1,0:T(8,128)(2,1)} %bitcast.16, ...), custom_call_target="tpu_custom_call" | custom-call | flops 134217728 | bytes 3145728 | tf_op jit(solution)/shard_map/local_part/pallas_call | solution.py:351
  11.4 0.3 %collective-permute-done.1.refs_7_ = bf16[512,128]{1,0:T(8,128)(2,1)S(1)} collective-permute-done((bf16[512,128]{1,0:T(8,128)(2,1)S(1)}, bf16[512,128]{1,0:T(8,128)(2,1)S(1)}, u32[]{:S(2)}, u32[]{:S(2)}) %collective-permute-start.1) | collective-permute-done | bytes 131104 | tf_op jit(solution)/shard_map/ppermute | solution.py:282
  11.7 1.0 %fold_part.1 = (s32[8,128]{1,0:T(8,128)S(1)}, f32[1024,128]{1,0:T(8,128)S(1)}, f32[1024,128]{1,0:T(8,128)S(1)}, f32[1024,128]{1,0:T(8,128)S(1)}) custom-call(s32[1,1]{1,0:T(1,128)} %bitcast.6.refs_0_, bf16[1024,256]{1,0:T(8,128)(2,1)S(1)} %get-tuple-element.40.refs_1_, f32[1024,128]{1,0:T(8,128)S(1)} %get-tuple-element.41.refs_2_, ...), custom_call_target="tpu_custom_call" | custom-call | flops 134217728 | bytes 3145728 | tf_op jit(solution)/shard_map/fold_part/pallas_call | solution.py:394
  12.7 1.7 %collective-permute-done.2.refs_6_ = bf16[512,128]{1,0:T(8,128)(2,1)S(1)} collective-permute-done((bf16[512,128]{1,0:T(8,128)(2,1)S(1)}, bf16[512,128]{1,0:T(8,128)(2,1)S(1)}, u32[]{:S(2)}, u32[]{:S(2)}) %collective-permute-start.2) | collective-permute-done | bytes 131104 | tf_op jit(solution)/shard_map/ppermute | solution.py:282
  14.4 1.5 %finish_part.1 = bf16[1024,128]{1,0:T(8,128)(2,1)} custom-call(s32[8,128]{1,0:T(8,128)S(1)} %get-tuple-element.47.refs_0_, bf16[1024,256]{1,0:T(8,128)(2,1)S(1)} %get-tuple-element.40.refs_1_, f32[1024,128]{1,0:T(8,128)S(1)} %get-tuple-element.48.refs_2_, f32[1024,128]{1,0:T(8,128)S(1)} %get-tuple-element.49.refs_3_, ...), custom_call_target="tpu_custom_call" | custom-call | flops 67108864 | bytes 3145728 | tf_op jit(solution)/shard_map/finish_part/pallas_call | solution.py:406
Async XLA Ops:
  0.0 4.1 %copy-start = (bf16[2,64,2,2,128]{4,3,2,1,0:T(2,128)(2,1)S(1)}, bf16[2,64,2,2,128]{4,3,2,1,0:T(2,128)(2,1)}, u32[]{:S(2)}) copy-start(bf16[2,64,2,2,128]{4,3,2,1,0:T(2,128)(2,1)} %param.8) | copy-start | bytes 393220
  0.0 7.9 %collective-permute-start = (bf16[512,128]{1,0:T(8,128)(2,1)}, bf16[512,128]{1,0:T(8,128)(2,1)S(1)}, u32[]{:S(2)}, u32[]{:S(2)}) collective-permute-start(bf16[512,128]{1,0:T(8,128)(2,1)} %bitcast.13), channel_id=1, source_target_pairs={{0,8},{8,12},{12,4},{4,0},{1,9},{9,13},{13,5},{5,1},{2,10},{10,14}... | collective-permute-start | bytes 393224 | tf_op jit(solution)/shard_map/ppermute | solution.py:282
  4.1 7.6 %collective-permute-start.1 = (bf16[512,128]{1,0:T(8,128)(2,1)S(1)}, bf16[512,128]{1,0:T(8,128)(2,1)S(1)}, u32[]{:S(2)}, u32[]{:S(2)}) collective-permute-start(bf16[512,128]{1,0:T(8,128)(2,1)S(1)} %bitcast.17), channel_id=1, source_target_pairs={{0,4},{8,0},{12,8},{4,12},{1,5},{9,1},{13,9},{5,13},{2,6},{10,2},{... | collective-permute-start | bytes 393224 | tf_op jit(solution)/shard_map/ppermute | solution.py:282
  7.9 6.5 %collective-permute-start.2 = (bf16[512,128]{1,0:T(8,128)(2,1)S(1)}, bf16[512,128]{1,0:T(8,128)(2,1)S(1)}, u32[]{:S(2)}, u32[]{:S(2)}) collective-permute-start(bf16[512,128]{1,0:T(8,128)(2,1)S(1)} %collective-permute-done.refs_6_), channel_id=1, source_target_pairs={{0,8},{8,12},{12,4},{4,0},{1,9},{9,13},{13,5},{5,1},{2,10},{10,14}... | collective-permute-start | bytes 393224 | tf_op jit(solution)/shard_map/ppermute | solution.py:282

commit v11 on v10

--- a/solution.py
+++ b/solution.py
@@ -186,7 +186,7 @@
 def my_turn():
     odd = lax.rem(lax.axis_index("tensor"), 2) == 1
     replica = lax.axis_index("replica")
-    first = lax.rem(replica, 2) == 1
+    first = replica != 2
     return jnp.where(
         odd, jnp.where(first, 0, 2), jnp.where(replica == 0, 1, 2)
     )

time: 16.1 us -> 16.1 us (level)
  transfers between devices with their start and end apart: 3 -> 3, of which waited for: 2 -> 1; matrix products, arithmetic and copies ran while one was open for 0% -> 0% of each run, Pallas kernels for 31% -> 31%
where the time goes in v11:
time: 16.1 us; the launch traced here: 16 us
  starting transfers between devices  6.67 us (41%)
  Pallas kernels  6.45 us (40%)
  waiting for transfers between devices  2.13 us (13%)
  between operations  0.72 us (4%)
    ppermute x3, starting transfers between devices, ring_step(): lax.ppermute(values, 'replica', [(ring[i], ring[(i + step) % len(ring)])...  6.67 us
    pallas_call x3, Pallas kernels, local_part(): pl.pallas_call(functools.partial(body, (heads, group, page, suffix, scale...  3.98 us
    ppermute x3, waiting for transfers between devices, ring_step(): lax.ppermute(values, 'replica', [(ring[i], ring[(i + step) % len(ring)])...  2.13 us
    pallas_call x1, Pallas kernels, shards(): pl.pallas_call(functools.partial(finish_body, sizes, place), out_shape=ja...  1.51 us
    pallas_call x1, Pallas kernels, shards(): pl.pallas_call(functools.partial(fold_body, sizes, place), out_shape=[jax...  0.96 us
  transfers between devices with their start and end apart: 3, of which 1 were waited for; matrix products, arithmetic and copies ran while one was open for 0% of the time, Pallas kernels for 31%

profile of v11, /device:TPU:0, one launch (start us, length us, event | category | flops | bytes accessed | tf_op | source)
XLA Modules:
  0.0 16.0 jit_solution(15322020871464328781)
XLA Ops:
  0.0 0.0 copy-start
  0.0 4.0 %collective-permute-start = (bf16[512,128]{1,0:T(8,128)(2,1)}, bf16[512,128]{1,0:T(8,128)(2,1)S(1)}, u32[]{:S(2)}, u32[]{:S(2)}) collective-permute-start(bf16[512,128]{1,0:T(8,128)(2,1)} %bitcast.13), channel_id=1, source_target_pairs={{0,8},{8,12},{12,4},{4,0},{1,9},{9,13},{13,5},{5,1},{2,10},{10,14}... | collective-permute-start | bytes 393224 | tf_op jit(solution)/shard_map/ppermute | solution.py:282
  4.0 0.1 local_part.3
  4.1 0.0 copy-done
  4.1 0.1 collective-permute-start.1
  4.2 3.7 %local_part.4 = (f32[1024,128]{1,0:T(8,128)S(1)}, f32[1024,128]{1,0:T(8,128)S(1)}, f32[1024,128]{1,0:T(8,128)S(1)}, bf16[1024,256]{1,0:T(8,128)(2,1)S(1)}, f32[8,384]{1,0:T(8,128)S(1)}) custom-call(s32[6]{0:T(128)} %refs_0_.5, s32[64]{0:T(128)} %refs_1_.5, bf16[1024,128]{1,0:T(8,128)(2,1)} %bitcast.11, bf16[512,128]{1,0:T(8,128)(2,1)} %bitcast.15, ...), custom_call_target="tpu_custom_call" | custom-call | flops 134217728 | bytes 3145728 | tf_op jit(solution)/shard_map/local_part/pallas_call | solution.py:351
  7.9 0.0 collective-permute-done.refs_6_
  7.9 2.6 %collective-permute-start.2 = (bf16[512,128]{1,0:T(8,128)(2,1)S(1)}, bf16[512,128]{1,0:T(8,128)(2,1)S(1)}, u32[]{:S(2)}, u32[]{:S(2)}) collective-permute-start(bf16[512,128]{1,0:T(8,128)(2,1)S(1)} %collective-permute-done.refs_6_), channel_id=1, source_target_pairs={{0,8},{8,12},{12,4},{4,0},{1,9},{9,13},{13,5},{5,1},{2,10},{10,14}... | collective-permute-start | bytes 393224 | tf_op jit(solution)/shard_map/ppermute | solution.py:282
  11.1 0.2 %local_part.5 = (f32[1024,128]{1,0:T(8,128)S(1)}, f32[1024,128]{1,0:T(8,128)S(1)}, f32[1024,128]{1,0:T(8,128)S(1)}, bf16[1024,256]{1,0:T(8,128)(2,1)S(1)}, f32[8,384]{1,0:T(8,128)S(1)}) custom-call(s32[6]{0:T(128)} %refs_0_.5, s32[64]{0:T(128)} %refs_1_.5, bf16[1024,128]{1,0:T(8,128)(2,1)} %bitcast.12, bf16[512,128]{1,0:T(8,128)(2,1)} %bitcast.16, ...), custom_call_target="tpu_custom_call" | custom-call | flops 134217728 | bytes 3145728 | tf_op jit(solution)/shard_map/local_part/pallas_call | solution.py:351
  11.4 0.0 collective-permute-done.1.refs_7_
  11.4 1.0 %fold_part.1 = (s32[8,128]{1,0:T(8,128)S(1)}, f32[1024,128]{1,0:T(8,128)S(1)}, f32[1024,128]{1,0:T(8,128)S(1)}, f32[1024,128]{1,0:T(8,128)S(1)}) custom-call(s32[1,1]{1,0:T(1,128)} %bitcast.6.refs_0_, bf16[1024,256]{1,0:T(8,128)(2,1)S(1)} %get-tuple-element.40.refs_1_, f32[1024,128]{1,0:T(8,128)S(1)} %get-tuple-element.41.refs_2_, ...), custom_call_target="tpu_custom_call" | custom-call | flops 134217728 | bytes 3145728 | tf_op jit(solution)/shard_map/fold_part/pallas_call | solution.py:394
  12.3 2.1 %collective-permute-done.2.refs_6_ = bf16[512,128]{1,0:T(8,128)(2,1)S(1)} collective-permute-done((bf16[512,128]{1,0:T(8,128)(2,1)S(1)}, bf16[512,128]{1,0:T(8,128)(2,1)S(1)}, u32[]{:S(2)}, u32[]{:S(2)}) %collective-permute-start.2) | collective-permute-done | bytes 131104 | tf_op jit(solution)/shard_map/ppermute | solution.py:282
  14.5 1.5 %finish_part.1 = bf16[1024,128]{1,0:T(8,128)(2,1)} custom-call(s32[8,128]{1,0:T(8,128)S(1)} %get-tuple-element.47.refs_0_, bf16[1024,256]{1,0:T(8,128)(2,1)S(1)} %get-tuple-element.40.refs_1_, f32[1024,128]{1,0:T(8,128)S(1)} %get-tuple-element.48.refs_2_, f32[1024,128]{1,0:T(8,128)S(1)} %get-tuple-element.49.refs_3_, ...), custom_call_target="tpu_custom_call" | custom-call | flops 67108864 | bytes 3145728 | tf_op jit(solution)/shard_map/finish_part/pallas_call | solution.py:406
Async XLA Ops:
  0.0 4.1 %copy-start = (bf16[2,64,2,2,128]{4,3,2,1,0:T(2,128)(2,1)S(1)}, bf16[2,64,2,2,128]{4,3,2,1,0:T(2,128)(2,1)}, u32[]{:S(2)}) copy-start(bf16[2,64,2,2,128]{4,3,2,1,0:T(2,128)(2,1)} %param.8) | copy-start | bytes 393220
  0.0 7.9 %collective-permute-start = (bf16[512,128]{1,0:T(8,128)(2,1)}, bf16[512,128]{1,0:T(8,128)(2,1)S(1)}, u32[]{:S(2)}, u32[]{:S(2)}) collective-permute-start(bf16[512,128]{1,0:T(8,128)(2,1)} %bitcast.13), channel_id=1, source_target_pairs={{0,8},{8,12},{12,4},{4,0},{1,9},{9,13},{13,5},{5,1},{2,10},{10,14}... | collective-permute-start | bytes 393224 | tf_op jit(solution)/shard_map/ppermute | solution.py:282
  4.1 7.2 %collective-permute-start.1 = (bf16[512,128]{1,0:T(8,128)(2,1)S(1)}, bf16[512,128]{1,0:T(8,128)(2,1)S(1)}, u32[]{:S(2)}, u32[]{:S(2)}) collective-permute-start(bf16[512,128]{1,0:T(8,128)(2,1)S(1)} %bitcast.17), channel_id=1, source_target_pairs={{0,4},{8,0},{12,8},{4,12},{1,5},{9,1},{13,9},{5,13},{2,6},{10,2},{... | collective-permute-start | bytes 393224 | tf_op jit(solution)/shard_map/ppermute | solution.py:282
  7.9 6.5 %collective-permute-start.2 = (bf16[512,128]{1,0:T(8,128)(2,1)S(1)}, bf16[512,128]{1,0:T(8,128)(2,1)S(1)}, u32[]{:S(2)}, u32[]{:S(2)}) collective-permute-start(bf16[512,128]{1,0:T(8,128)(2,1)S(1)} %collective-permute-done.refs_6_), channel_id=1, source_target_pairs={{0,8},{8,12},{12,4},{4,0},{1,9},{9,13},{13,5},{5,1},{2,10},{10,14}... | collective-permute-start | bytes 393224 | tf_op jit(solution)/shard_map/ppermute | solution.py:282
